TPU v7x, 256 devices: a whole 4x4x8 slice. The times are simulated.
256 devices in a mesh: gx: 64 (over y, z, core), gy: 4 (over x).
Axes of the slice: x: 4, y: 4, z: 8, core: 2. Of those that a mesh axis runs over, the one named last changes fastest.
Arguments:
- query: bfloat16 [256, 16384], P('gx', 'gy'), may hold values from -48 to 48
- key_cache: bfloat16 [256, 8, 256, 128], P('gx', 'gy'), may hold values from -13 to 13
- value_cache: bfloat16 [256, 8, 256, 128], P('gx', 'gy'), may hold values from -5 to 5
- key_new: bfloat16 [256, 1024], P('gx', 'gy'), may hold values from -13 to 13
- value_new: bfloat16 [256, 1024], P('gx', 'gy'), may hold values from -5 to 5
- lengths: int32 [256], P('gx'), may hold values from 1 to 256, as said below
- residual_in: bfloat16 [256, 16384], P(None, ('gy', 'gx')), may hold values from -24 to 24
- out_weight: bfloat16 [16384, 16384], P(None, ('gy', 'gx')), may hold values from -0.046875 to 0.046875
- norm_gain: bfloat16 [16384], P(('gy', 'gx')), may hold values from 0.25 to 1.75
- gate_weight: bfloat16 [16384, 26624], P('gy', 'gx'), may hold values from -0.046875 to 0.046875
- up_weight: bfloat16 [16384, 26624], P('gy', 'gx'), may hold values from -0.046875 to 0.046875
- down_weight: bfloat16 [26624, 16384], P('gx', 'gy'), may hold values from -0.109375 to 0.109375
Outputs:
- layer_out: bfloat16 [256, 16384], P(None, ('gy', 'gx'))
Inputs may be any that keep to these rules, and one draw needn't show every extreme that they name: `lengths`: some row has exactly 256 valid positions and some row exactly 1.
All inputs are finite; a program needn't handle non-finite values.
Results may differ from a plain program's by a relative error of at most 0.007.
Values may be sent and summed in bfloat16 or wider, within the bound.
No kernel may reach another device: no remote copies, remote signals or barrier semaphores. Data moves between devices by JAX's collectives and lax.ppermute only.
A program may use at most 128 MiB of HBM per device.

v0:
```python
import jax
import jax.numpy as jnp
from jax import lax
from jax.sharding import PartitionSpec as P

D = 16384


def attend(query, key_cache, value_cache, key_new, value_new, lengths):
    row_count = query.shape[0]
    kv_heads = key_cache.shape[1]
    context = key_cache.shape[2]
    head_size = key_cache.shape[3]
    group_size = query.shape[1] // (kv_heads * head_size)
    query_rows = query.reshape(row_count, kv_heads, group_size, head_size)
    incoming_keys = key_new.reshape(row_count, kv_heads, head_size)
    fresh_values = value_new.astype(jnp.float32).reshape(row_count, kv_heads, head_size)
    logit_scale = head_size ** (-0.5)
    cache_scores = (
        jnp.einsum("bkgd,bktd->bkgt", query_rows, key_cache, preferred_element_type=jnp.float32)
        * logit_scale
    )
    incoming_scores = (
        jnp.einsum("qaxh,qah->qax", query_rows, incoming_keys, preferred_element_type=jnp.float32)
        * logit_scale
    )
    valid = lax.broadcasted_iota(jnp.int32, (row_count, context), 1) < lengths[:, None]
    cache_scores = jnp.where(valid[:, None, None, :], cache_scores, -1e30)
    peak = jnp.maximum(jnp.max(cache_scores, axis=3), incoming_scores)
    cache_weights = jnp.exp(cache_scores - peak[..., None])
    new_weight = jnp.exp(incoming_scores - peak)
    denominator = jnp.sum(cache_weights, axis=3) + new_weight
    cache_low = cache_weights.astype(jnp.bfloat16)
    new_low = new_weight.astype(jnp.bfloat16).astype(jnp.float32)
    weighted_value_sum = jnp.einsum(
        "bkgt,bktd->bkgd", cache_low, value_cache, preferred_element_type=jnp.float32
    )
    weighted_value_sum = weighted_value_sum + new_low[..., None] * fresh_values[:, :, None, :]
    attended = (weighted_value_sum / denominator[..., None]).astype(jnp.bfloat16)
    return attended.reshape(row_count, kv_heads * group_size * head_size)


def per_device(
    query,
    key_cache,
    value_cache,
    key_new,
    value_new,
    lengths,
    residual_in,
    out_weight,
    norm_gain,
    gate_weight,
    up_weight,
    down_weight,
):
    attended = attend(query, key_cache, value_cache, key_new, value_new, lengths)
    widened = lax.all_gather(attended, "gy", axis=1, tiled=True)
    projected = jnp.dot(
        lax.all_gather(widened, "gx", axis=0, tiled=True),
        out_weight,
        preferred_element_type=jnp.float32,
    )
    hsum = residual_in.astype(jnp.float32) + projected
    square_sums = lax.psum(jnp.sum(hsum * hsum, axis=1), ("gx", "gy"))
    inverse = lax.rsqrt(square_sums[:, None] / D + 1e-05)
    normed = (hsum * inverse * norm_gain.astype(jnp.float32)[None, :]).astype(jnp.bfloat16)
    piece = lax.all_gather(normed, "gx", axis=1, tiled=True)
    gate = jnp.dot(piece, gate_weight, preferred_element_type=jnp.float32)
    up = jnp.dot(piece, up_weight, preferred_element_type=jnp.float32)
    gate, up = lax.psum((gate, up), "gy")
    hidden = (jax.nn.silu(gate) * up).astype(jnp.bfloat16)
    terms = jnp.dot(hidden, down_weight, preferred_element_type=jnp.float32)
    branch = lax.psum_scatter(terms, "gx", scatter_dimension=1, tiled=True)
    return (hsum + branch).astype(jnp.bfloat16)


def solution(mesh):
    placed = (
        P("gx", "gy"),
        P("gx", "gy", None, None),
        P("gx", "gy", None, None),
        P("gx", "gy"),
        P("gx", "gy"),
        P("gx"),
        P(None, ("gy", "gx")),
        P(None, ("gy", "gx")),
        P(("gy", "gx")),
        P("gy", "gx"),
        P("gy", "gx"),
        P("gx", "gy"),
    )
    return jax.shard_map(
        per_device, mesh=mesh, in_specs=placed, out_specs=P(None, ("gy", "gx")), check_vma=False
    )
```

profile of v0, /device:TPU:1, one launch (start us, length us, event | category | flops | bytes accessed | tf_op | source)
XLA Modules:
  0.0 488.3 jit_solution(3147993425818308279)
XLA Ops:
  6.5 0.0 copy-start
  6.5 0.0 all-gather.6.cloned.1.call-start
  6.5 0.9 copy.15
  7.5 0.0 copy-start.1
  7.5 0.9 iota_compare_fusion
  8.3 0.7 reshape.42
  9.0 0.0 copy-done.1
  9.0 0.1 fusion.12
  9.1 1.4 fusion.11
  10.5 0.2 fusion.5
  10.8 0.7 reshape.36
  11.5 1.3 fusion.2
  12.8 11.3 %all_gather.9 = bf16[4,16384]{1,0:T(4,128)(2,1)} all-gather(bf16[4,4096]{1,0:T(4,128)(2,1)S(1)} %bitcast.24), channel_id=1, replica_groups=mesh['gx'=64,'gy'=4] {'gy'}, dimensions={1}, use_global_device_ids=true | all-gather | bytes 163840 | tf_op jit(solution)/shard_map/all_gather | solution.py:58
  24.1 0.0 all-gather.6.cloned.1.call-update
  24.1 0.0 all-gather.4.cloned.1.call-start
  24.2 0.7 convert_element_type.33
  24.8 0.0 copy-start.2
  24.9 87.9 %all-gather.6.cloned.1.call-done = bf16[64,4,16384]{2,1,0:T(4,128)(2,1)} async-done(((bf16[1,4,16384]{2,1,0:T(4,128)(2,1)}), bf16[64,4,16384]{2,1,0:T(4,128)(2,1)}) %all-gather.6.cloned.1.call-update) | async-done | bytes 8388624 | tf_op jit(solution)/shard_map/all_gather | solution.py:60
  112.7 12.5 %reshape.38 = bf16[256,16384]{1,0:T(8,128)(2,1)} reshape(bf16[64,4,16384]{2,1,0:T(4,128)(2,1)} %all-gather.6.cloned.1.call-done) | data formatting | bytes 16777216
  125.2 0.0 copy-done.2
  125.3 6.7 %multiply_reduce_fusion = (f32[256]{0:T(256)S(1)}, f32[256,64]{0,1:T(8,128)S(1)}) fusion(bf16[256,16384]{1,0:T(8,128)(2,1)} %reshape.38, bf16[16384,64]{0,1:T(8,128)(2,1)} %param.19, bf16[256,64]{0,1:T(8,128)(2,1)S(1)} %copy-done.2), kind=kOutput, calls=%fused_computation.14 | convolution fusion | flops 536936192 | bytes 10585088 | tf_op jit(solution)/shard_map/dot_general | solution.py:59
  131.9 75.0 %psum.21 = f32[256]{0:T(256)S(1)} all-reduce(f32[256]{0:T(256)S(1)} %get-tuple-element.11), channel_id=1, replica_groups=mesh['gx'=64,'gy'=4] {'gx','gy'}, use_global_device_ids=true, to_apply=%region_3.4 | all-reduce | flops 256 | bytes 2048 | tf_op jit(solution)/shard_map/psum | solution.py:65
  206.9 0.7 multiply_convert_fusion.2
  207.6 0.0 all-gather.4.cloned.1.call-update
  207.6 0.0 all-reduce.3.cloned.1.call-start
  207.6 74.2 %all-gather.4.cloned.1.call-done = bf16[256,4096]{0,1:T(8,128)(2,1)} async-done(((bf16[256,64]{0,1:T(8,128)(2,1)}), bf16[256,4096]{0,1:T(8,128)(2,1)}) %all-gather.4.cloned.1.call-update) | async-done | bytes 2097168 | tf_op jit(solution)/shard_map/all_gather | solution.py:68
  281.8 0.0 copy-start.3
  281.8 0.0 copy-start.4
  281.8 4.6 fusion.13
  286.4 0.0 copy-done.3
  286.4 0.0 copy-done.4
  286.4 1.8 fusion.14
  288.2 0.0 all-reduce.3.cloned.1.call-update
  288.2 0.0 reduce-scatter.2.cloned.1.call-start
  288.3 45.5 %all-reduce.3.cloned.1.call-done = (f32[256,416]{0,1:T(8,128)}, f32[256,416]{0,1:T(8,128)}) async-done(((f32[256,416]{0,1:T(8,128)}, f32[256,416]{0,1:T(8,128)}), (f32[256,416]{0,1:T(8,128)}, f32[256,416]{0,1:T(8,128)})) %all-reduce.3.cloned.1.call-update) | async-done | bytes 851984 | tf_op jit(solution)/shard_map/psum | solution.py:71
  333.8 0.0 copy-done
  333.8 4.8 fusion.3
  338.7 0.0 reduce-scatter.2.cloned.1.call-update
  338.7 141.6 %reduce-scatter.2.cloned.1.call-done = f32[256,64]{0,1:T(8,128)} async-done(((f32[256,4096]{0,1:T(8,128)}), f32[256,64]{0,1:T(8,128)}) %reduce-scatter.2.cloned.1.call-update) | async-done | bytes 65552 | tf_op jit(solution)/shard_map/reduce_scatter | solution.py:74
  480.3 1.5 add_convert_fusion
  (4 shorter events, 0.1 us)
Async XLA Ops:
  6.5 327.3 %copy-start = (bf16[416,4096]{1,0:T(8,128)(2,1)S(1)}, bf16[416,4096]{1,0:T(8,128)(2,1)}, u32[]{:S(2)}) copy-start(bf16[416,4096]{1,0:T(8,128)(2,1)} %param.23) | copy-start | bytes 10223620
  6.5 106.2 %all-gather.6.cloned.1.call-start = ((), (), s32[]{:S(2)}) async-start(), calls=%async_computation.3 | async-start | bytes 8519680 | tf_op jit(solution)/shard_map/all_gather | solution.py:60
  7.5 1.6 copy-start.1
  24.1 257.7 %all-gather.4.cloned.1.call-start = ((), (), s32[]{:S(2)}) async-start(), calls=%async_computation.1 | async-start | bytes 2129920 | tf_op jit(solution)/shard_map/all_gather | solution.py:68
  24.8 100.4 %copy-start.2 = (bf16[256,64]{0,1:T(8,128)(2,1)S(1)}, bf16[256,64]{0,1:T(8,128)(2,1)}, u32[]{:S(2)}) copy-start(bf16[256,64]{0,1:T(8,128)(2,1)} %param.18) | copy-start | bytes 98308
  207.6 126.2 %all-reduce.3.cloned.1.call-start = ((), (), s32[]{:S(2)}) async-start(), calls=%async_computation.4 | async-start | bytes 1703936 | tf_op jit(solution)/shard_map/psum | solution.py:71
  281.8 4.6 copy-start.3
  281.8 4.6 copy-start.4
  288.2 192.0 %reduce-scatter.2.cloned.1.call-start = ((), (), s32[]{:S(2)}) async-start(), calls=%async_computation.2 | async-start | bytes 4259840 | tf_op jit(solution)/shard_map/reduce_scatter | solution.py:74
Sparse Core Ops, SparseCore 0:
  24.3 88.4 all-gather.5
  207.7 74.0 all-gather.3
  288.4 45.4 all-reduce.2
  338.8 141.4 reduce-scatter.1
where the time goes:
time: 493 us; the launch traced here: 488 us
  waiting for transfers between devices  349 us (71%)
  blocking collectives  86.3 us (18%)
  matrix products  20.7 us (4%)
  local copies, waits for them, and re-layouts  14.9 us (3%)
  between operations  13.2 us (3%)
    reduce_scatter x1, waiting for transfers between devices, per_device(): branch = lax.psum_scatter(terms, 'gx', scatter_dimension=1, tiled=True)  142 us
    all_gather x1, waiting for transfers between devices, per_device(): lax.all_gather(widened, 'gx', axis=0, tiled=True)  87.9 us
    psum x1, blocking collectives, per_device(): square_sums = lax.psum(jnp.sum(hsum * hsum, axis=1), ('gx', 'gy'))  75 us
    all_gather x1, waiting for transfers between devices, per_device(): piece = lax.all_gather(normed, 'gx', axis=1, tiled=True)  74.2 us
    psum x1, waiting for transfers between devices, per_device(): gate, up = lax.psum((gate, up), 'gy')  45.5 us
    unnamed x13, local copies, waits for them, and re-layouts  13.5 us
    all_gather x1, blocking collectives, per_device(): widened = lax.all_gather(attended, 'gy', axis=1, tiled=True)  11.3 us
  transfers between devices with their start and end apart: 4, of which 4 were waited for; matrix products, arithmetic and copies ran while one was open for 0% of the time, Pallas kernels for 0%

commit v1 on v0

v1 whole, which is shorter than its diff:
```python
import jax
import jax.numpy as jnp
import numpy as np
from jax import lax
from jax.sharding import PartitionSpec as P

D = 16384
PLANE = 32
CORES = 2
QUARTERS = 4
ROWS_HERE = 4

F32 = jnp.float32
BF16 = jnp.bfloat16


def row_order():
    row = np.arange(PLANE * CORES * ROWS_HERE)
    device, inner = row // ROWS_HERE, row % ROWS_HERE
    place = (device % CORES) * (PLANE * ROWS_HERE) + (device // CORES) * ROWS_HERE + inner
    table = np.zeros((row.size, row.size), np.float32)
    table[row, place] = 1.0
    return table


def to_core(value):
    return lax.ppermute(value, "gx", [(g, g ^ 1) for g in range(PLANE * CORES)])


def along_gy(value, step):
    return lax.ppermute(value, "gy", [(i, (i + step) % QUARTERS) for i in range(QUARTERS)])


def plane_exchange(blocks):
    groups = [[p * CORES + c for p in range(PLANE)] for c in range(CORES)]
    return lax.all_to_all(blocks, "gx", 0, 0, axis_index_groups=groups, tiled=True)


def attend(query, key_cache, value_cache, key_new, value_new, lengths):
    row_count = query.shape[0]
    kv_heads = key_cache.shape[1]
    context = key_cache.shape[2]
    head_size = key_cache.shape[3]
    group_size = query.shape[1] // (kv_heads * head_size)
    query_rows = query.reshape(row_count, kv_heads, group_size, head_size)
    incoming_keys = key_new.reshape(row_count, kv_heads, head_size)
    fresh_values = value_new.astype(F32).reshape(row_count, kv_heads, head_size)
    logit_scale = head_size ** (-0.5)
    cache_scores = (
        jnp.einsum("bkgd,bktd->bkgt", query_rows, key_cache, preferred_element_type=F32)
        * logit_scale
    )
    incoming_scores = (
        jnp.einsum("qaxh,qah->qax", query_rows, incoming_keys, preferred_element_type=F32)
        * logit_scale
    )
    valid = lax.broadcasted_iota(jnp.int32, (row_count, context), 1) < lengths[:, None]
    cache_scores = jnp.where(valid[:, None, None, :], cache_scores, -1e30)
    peak = jnp.maximum(jnp.max(cache_scores, axis=3), incoming_scores)
    cache_weights = jnp.exp(cache_scores - peak[..., None])
    new_weight = jnp.exp(incoming_scores - peak)
    denominator = jnp.sum(cache_weights, axis=3) + new_weight
    cache_low = cache_weights.astype(BF16)
    new_low = new_weight.astype(BF16).astype(F32)
    weighted_value_sum = jnp.einsum(
        "bkgt,bktd->bkgd", cache_low, value_cache, preferred_element_type=F32
    )
    weighted_value_sum = weighted_value_sum + new_low[..., None] * fresh_values[:, :, None, :]
    attended = (weighted_value_sum / denominator[..., None]).astype(BF16)
    return attended.reshape(row_count, kv_heads * group_size * head_size)


def pair_order(own, other, core):
    return jnp.where(
        core == 0, jnp.concatenate([own, other], 0), jnp.concatenate([other, own], 0)
    )


def per_device(
    query,
    key_cache,
    value_cache,
    key_new,
    value_new,
    lengths,
    residual_in,
    out_weight,
    norm_gain,
    gate_weight,
    up_weight,
    down_weight,
):
    core = lax.axis_index("gx") % CORES
    quarter = lax.axis_index("gy")
    order = jnp.asarray(row_order(), BF16)
    width = out_weight.shape[0] // QUARTERS
    columns = out_weight.shape[1]
    half = PLANE * ROWS_HERE

    out_rows = out_weight.T
    own_out = [lax.dynamic_slice_in_dim(out_rows, quarter * width, width, 1)]
    for step in range(1, QUARTERS):
        to = (quarter + step) % QUARTERS
        own_out.append(along_gy(lax.dynamic_slice_in_dim(out_rows, to * width, width, 1), step))
    own_out = jnp.concatenate(own_out, 0)

    gate_other, up_other = to_core(gate_weight.T), to_core(up_weight.T)
    down_other = to_core(down_weight)

    residual = jnp.dot(residual_in.T, order, preferred_element_type=F32).astype(BF16)
    gain = jnp.broadcast_to(norm_gain[:, None], (columns, half))
    mine = lax.dynamic_slice_in_dim(residual, core * half, half, 1)
    theirs = lax.dynamic_slice_in_dim(residual, (1 - core) * half, half, 1)
    received = to_core(jnp.concatenate([theirs, gain], 1))
    residual = pair_order(mine, received[:, :half], core).astype(F32)
    gain = pair_order(gain, received[:, half:], core).astype(F32)

    attended = attend(query, key_cache, value_cache, key_new, value_new, lengths)
    gathered = plane_exchange(jnp.broadcast_to(attended[None], (PLANE,) + attended.shape))
    rows = gathered.reshape(half, width)

    other_out = to_core(own_out)

    def project(weights):
        return lax.dot_general(
            weights, rows, (((1,), (1,)), ((), ())), preferred_element_type=F32
        ).reshape(QUARTERS, columns, half)

    own_part, other_part = project(own_out), project(other_out)
    parts = jnp.where(
        core == 0,
        jnp.concatenate([own_part, other_part], 1),
        jnp.concatenate([other_part, own_part], 1),
    )
    projected = parts[0]
    for step in range(1, QUARTERS):
        projected = projected + along_gy(parts[step].astype(BF16), -step).astype(F32)
    hsum = residual + projected

    squares = jnp.sum(hsum * hsum, axis=0, keepdims=True)
    high = squares.astype(BF16)
    low = (squares - high.astype(F32)).astype(BF16)
    block = jnp.concatenate(
        [(hsum * gain).astype(BF16), high, low, jnp.zeros((14, half), BF16)], 0
    )
    blocks = plane_exchange(jnp.broadcast_to(block[None], (PLANE,) + block.shape))
    features = blocks[:, : CORES * columns].reshape(width, half)
    squares = jnp.sum(blocks[:, 128].astype(F32) + blocks[:, 129].astype(F32), axis=0)

    units = gate_weight.shape[1] // 2
    def expand(weights):
        return jnp.dot(weights, features, preferred_element_type=F32).reshape(2, units, half)

    gates = jnp.concatenate([expand(gate_weight.T), expand(gate_other)], 0)
    ups = jnp.concatenate([expand(up_weight.T), expand(up_other)], 0)
    high = squares.astype(BF16)
    low = (squares - high.astype(F32)).astype(BF16)
    tail = jnp.concatenate([high[None], low[None], jnp.zeros((14, half), BF16)], 0)
    tail = jnp.broadcast_to(tail[None], (QUARTERS,) + tail.shape)
    sends = jnp.concatenate([gates.astype(BF16), ups.astype(BF16), tail], 1)

    def chunk_of(to):
        return ((to // 2) ^ core) * 2 + to % 2

    total = lax.dynamic_index_in_dim(sends, chunk_of(quarter), 0, False).astype(F32)
    for step in range(1, QUARTERS):
        to = (quarter + step) % QUARTERS
        part = lax.dynamic_index_in_dim(sends, chunk_of(to), 0, False)
        total = total + along_gy(part, step).astype(F32)
    squares = total[2 * units : 2 * units + 1] + total[2 * units + 1 : 2 * units + 2]
    inverse = lax.rsqrt(squares / D + 1e-05)
    gate = total[:units] * inverse
    up = total[units : 2 * units] * inverse
    hidden = (jax.nn.silu(gate) * up).astype(BF16)

    chunks = jnp.stack([hidden] + [along_gy(hidden, step) for step in range(1, QUARTERS)])
    ordered = [
        lax.dynamic_index_in_dim(
            chunks, (quarter - (((place // 2) ^ core) * 2 + place % 2)) % QUARTERS, 0, False
        )
        for place in range(QUARTERS)
    ]
    hidden = jnp.concatenate(ordered, 0)

    def contract(weights, values):
        return lax.dot_general(
            weights, values, (((0,), (0,)), ((), ())), preferred_element_type=F32
        )

    branch = contract(down_weight, hidden[: 2 * units]) + contract(down_other, hidden[2 * units :])
    branch = branch.astype(BF16).reshape(PLANE, CORES * columns, half)
    branch = jnp.sum(plane_exchange(branch).astype(F32), axis=0)

    out = (hsum + branch).astype(BF16)
    mine = lax.dynamic_slice_in_dim(out, core * columns, columns, 0)
    theirs = to_core(lax.dynamic_slice_in_dim(out, (1 - core) * columns, columns, 0))
    out = jnp.where(
        core == 0,
        jnp.concatenate([mine, theirs], 1),
        jnp.concatenate([theirs, mine], 1),
    )
    out = lax.dot_general(order, out, (((1,), (1,)), ((), ())), preferred_element_type=F32)
    return out.astype(BF16)


def solution(mesh):
    placed = (
        P("gx", "gy"),
        P("gx", "gy", None, None),
        P("gx", "gy", None, None),
        P("gx", "gy"),
        P("gx", "gy"),
        P("gx"),
        P(None, ("gy", "gx")),
        P(None, ("gy", "gx")),
        P(("gy", "gx")),
        P("gy", "gx"),
        P("gy", "gx"),
        P("gx", "gy"),
    )
    return jax.shard_map(
        per_device, mesh=mesh, in_specs=placed, out_specs=P(None, ("gy", "gx")), check_vma=False
    )
```

time: 493 us -> 163 us (0.33)
  waiting for transfers between devices: 349 us -> 71.6 us
  blocking collectives: 86.3 us -> 0 us
  starting transfers between devices: 0.13 us -> 57.2 us
  between operations: 13.2 us -> 0.5 us
  local copies, waits for them, and re-layouts: 14.9 us -> 7.3 us
    all_gather x2 -> x0, waiting for transfers between devices: 162 us -> none  [the longest x1 87.9 us: per_device(): lax.all_gather(widened, 'gx', axis=0, tiled=True)]
    reduce_scatter x1 -> x0, waiting for transfers between devices: 142 us -> none  [per_device(): branch = lax.psum_scatter(terms, 'gx', scatter_dimension=1, tiled=True)]
    psum x1 -> x0, blocking collectives: 75 us -> none  [per_device(): square_sums = lax.psum(jnp.sum(hsum * hsum, axis=1), ('gx', 'gy'))]
    all_to_all x0 -> x3, waiting for transfers between devices: none -> 52.8 us  [plane_exchange(): lax.all_to_all(blocks, 'gx', 0, 0, axis_index_groups=groups, tiled=True)]
    psum x1 -> x0, waiting for transfers between devices: 45.5 us -> none  [per_device(): gate, up = lax.psum((gate, up), 'gy')]
    ppermute x0 -> x18, starting transfers between devices: none -> 29.4 us  [the longest x6 14.7 us: to_core(): return lax.ppermute(value, 'gx', [(g, g ^ 1) for g in range(PLANE * CORES)])]
    all_to_all x0 -> x3, starting transfers between devices: none -> 27.8 us  [plane_exchange(): lax.all_to_all(blocks, 'gx', 0, 0, axis_index_groups=groups, tiled=True)]
    ppermute x0 -> x18, waiting for transfers between devices: none -> 18.8 us  [the longest x12 17.9 us: along_gy(): lax.ppermute(value, 'gy', [(i, (i + step) % QUARTERS) for i in range(QUAR...]
  transfers between devices with their start and end apart: 4 -> 21, of which waited for: 4 -> 12; matrix products, arithmetic and copies ran while one was open for 0% -> 15% of each run, Pallas kernels for 0% -> 0%
where the time goes in v1:
time: 163 us; the launch traced here: 162 us
  waiting for transfers between devices  71.6 us (44%)
  starting transfers between devices  57.2 us (35%)
  matrix products  21.9 us (13%)
  local copies, waits for them, and re-layouts  7.3 us (4%)
  other arithmetic  3.77 us (2%)
    all_to_all x3, waiting for transfers between devices, plane_exchange(): lax.all_to_all(blocks, 'gx', 0, 0, axis_index_groups=groups, tiled=True)  52.8 us
    all_to_all x3, starting transfers between devices, plane_exchange(): lax.all_to_all(blocks, 'gx', 0, 0, axis_index_groups=groups, tiled=True)  27.8 us
    ppermute x12, waiting for transfers between devices, along_gy(): lax.ppermute(value, 'gy', [(i, (i + step) % QUARTERS) for i in range(QUAR...  17.9 us
    ppermute x6, starting transfers between devices, to_core(): return lax.ppermute(value, 'gx', [(g, g ^ 1) for g in range(PLANE * CORES)])  14.7 us
    ppermute x12, starting transfers between devices, along_gy(): lax.ppermute(value, 'gy', [(i, (i + step) % QUARTERS) for i in range(QUAR...  14.7 us
    dot_general x4, matrix products, expand(): jnp.dot(weights, features, preferred_element_type=F32)  10.2 us
    dot_general x2, matrix products, contract(): lax.dot_general(weights, values, (((0,), (0,)), ((), ())), preferred_elem...  5.44 us
    dot_general x2, matrix products, project(): lax.dot_general(weights, rows, (((1,), (1,)), ((), ())), preferred_elemen...  4.59 us
  transfers between devices with their start and end apart: 21, of which 12 were waited for; matrix products, arithmetic and copies ran while one was open for 15% of the time, Pallas kernels for 0%

profile of v1, /device:TPU:1, one launch (start us, length us, event | category | flops | bytes accessed | tf_op | source)
XLA Modules:
  0.0 162.3 jit_solution(14542083205306444340)
XLA Ops:
  0.1 2.6 %dynamic-slice_bitcast_fusion.3 = (bf16[64,4096]{1,0:T(8,128)(2,1)S(1)}, bf16[64,4096]{1,0:T(8,128)(2,1)}, bf16[64,4096]{1,0:T(8,128)(2,1)S(1)}, bf16[64,4096]{1,0:T(8,128)(2,1)S(1)}) fusion(bf16[16384,64]{0,1:T(8,128)(2,1)} %param.20, s32[]{:T(128)S(6)} %select_n.159, s32[]{:T(128)S(6)} %select_n.161, s32[]{:T(128)S(6)} %select_n.165, s32[]{:T(128)S(6)} %select_n.163), kind=kLoop, calls=%fused_computation.21 | loop fusion | bytes 4194320 | tf_op jit(solution)/shard_map/dynamic_slice | solution.py:101
  2.7 2.0 %collective-permute-start.1 = (bf16[64,4096]{1,0:T(8,128)(2,1)}, bf16[64,4096]{1,0:T(8,128)(2,1)}, u32[]{:S(2)}, u32[]{:S(2)}) collective-permute-start(bf16[64,4096]{1,0:T(8,128)(2,1)} %get-tuple-element.10), channel_id=1, source_target_pairs={{0,1},{1,2},{2,3},{3,0},{4,5},{5,6},{6,7},{7,4},{8,9},{9,10},{10,1... | collective-permute-start | bytes 1572872 | tf_op jit(solution)/shard_map/ppermute | solution.py:31
  4.7 1.3 collective-permute-start.3
  6.0 1.7 %collective-permute-start.2 = (bf16[64,4096]{1,0:T(8,128)(2,1)S(1)}, bf16[64,4096]{1,0:T(8,128)(2,1)}, u32[]{:S(2)}, u32[]{:S(2)}) collective-permute-start(bf16[64,4096]{1,0:T(8,128)(2,1)S(1)} %get-tuple-element.12), channel_id=1, source_target_pairs={{0,2},{1,3},{2,0},{3,1},{4,6},{5,7},{6,4},{7,5},{8,10},{9,11},{10,... | collective-permute-start | bytes 1572872 | tf_op jit(solution)/shard_map/ppermute | solution.py:31
  7.9 0.3 fusion.42
  8.3 0.2 fusion.8
  8.5 0.2 fusion.4
  8.8 1.5 broadcast_in_dim.26
  10.3 11.3 %all-to-all-start = ((bf16[32,4,4096]{2,1,0:T(4,128)(2,1)}), bf16[32,4,4096]{2,1,0:T(4,128)(2,1)S(1)}, u32[]{:S(2)}, u32[]{:S(2)}) async-start(bf16[32,4,4096]{2,1,0:T(4,128)(2,1)} %broadcast_in_dim.26), calls=%async_computation | async-start | bytes 2097152 | tf_op jit(solution)/shard_map/all_to_all | solution.py:36
  21.7 8.3 %collective-permute-done.2 = bf16[64,4096]{1,0:T(8,128)(2,1)} collective-permute-done((bf16[64,4096]{1,0:T(8,128)(2,1)S(1)}, bf16[64,4096]{1,0:T(8,128)(2,1)}, u32[]{:S(2)}, u32[]{:S(2)}) %collective-permute-start.2) | collective-permute-done | bytes 524320 | tf_op jit(solution)/shard_map/ppermute | solution.py:31
  30.0 2.9 %pad_maximum_fusion = bf16[256,4096]{1,0:T(8,128)(2,1)} fusion(bf16[64,4096]{1,0:T(8,128)(2,1)} %collective-permute-done.3, bf16[64,4096]{1,0:T(8,128)(2,1)} %collective-permute-done.2, bf16[64,4096]{1,0:T(8,128)(2,1)} %collective-permute-done.1, bf16[64,4096]{1,0:T(8,128)(2,1)S(1)} %get-tuple-element.9), kind=kLoop, calls=%fused_computation.2 | loop fusion | flops 8388608 | bytes 4194304 | tf_op jit(solution)/shard_map/concatenate | solution.py:105
  33.0 1.5 collective-permute-start.4
  34.9 11.3 %all-to-all-done = bf16[32,4,4096]{2,1,0:T(4,128)(2,1)S(1)} async-done(((bf16[32,4,4096]{2,1,0:T(4,128)(2,1)}), bf16[32,4,4096]{2,1,0:T(4,128)(2,1)S(1)}, u32[]{:S(2)}, u32[]{:S(2)}) %all-to-all-start) | async-done | bytes 1048608 | tf_op jit(solution)/shard_map/all_to_all | solution.py:36
  46.1 0.3 reshape.123
  46.4 2.3 %fusion.44 = f32[4,64,128]{2,1,0:T(8,128)S(1)} fusion(bf16[4,64,4096]{2,1,0:T(8,128)(2,1)} %bitcast.6, bf16[128,4096,1]{1,0,2:T(8,128)(2,1)S(1)} %reshape.123), kind=kOutput, calls=%fused_computation.101 | convolution fusion | flops 268435456 | bytes 3276800 | tf_op jit(solution)/shard_map/dot_general | solution.py:125
  48.7 2.3 %fusion.45 = f32[4,64,128]{2,1,0:T(8,128)S(1)} fusion(bf16[4,64,4096]{2,1,0:T(8,128)(2,1)} %bitcast.9, bf16[128,4096,1]{1,0,2:T(8,128)(2,1)S(1)} %reshape.123), kind=kOutput, calls=%fused_computation.102 | convolution fusion | flops 268435456 | bytes 3276800 | tf_op jit(solution)/shard_map/dot_general | solution.py:125
  51.1 0.9 collective-permute-start.5
  52.0 0.6 collective-permute-start.7
  52.6 1.4 collective-permute-start.6
  54.1 1.9 %collective-permute-done.7 = bf16[128,128]{1,0:T(8,128)(2,1)S(1)} collective-permute-done((bf16[128,128]{1,0:T(8,128)(2,1)S(1)}, bf16[128,128]{1,0:T(8,128)(2,1)S(1)}, u32[]{:S(2)}, u32[]{:S(2)}) %collective-permute-start.7) | collective-permute-done | bytes 32800 | tf_op jit(solution)/shard_map/ppermute | solution.py:31
  56.0 0.9 collective-permute-done.6
  57.0 1.2 broadcast_in_dim.27
  58.2 8.8 %all-to-all-start.1 = ((bf16[32,144,128]{2,1,0:T(8,128)(2,1)}), bf16[32,144,128]{2,1,0:T(8,128)(2,1)S(1)}, u32[]{:S(2)}, u32[]{:S(2)}) async-start(bf16[32,144,128]{2,1,0:T(8,128)(2,1)} %broadcast_in_dim.27), calls=%async_computation.1 | async-start | bytes 2359296 | tf_op jit(solution)/shard_map/all_to_all | solution.py:36
  67.0 3.2 %collective-permute-start.9 = (bf16[416,4096]{1,0:T(8,128)(2,1)}, bf16[416,4096]{1,0:T(8,128)(2,1)}, u32[]{:S(2)}, u32[]{:S(2)}) collective-permute-start(bf16[416,4096]{1,0:T(8,128)(2,1)} %bitcast.142), channel_id=1, source_target_pairs={{0,4},{4,0},{8,12},{12,8},{16,20},{20,16},{24,28},{28,24},{32,36},... | collective-permute-start | bytes 10223624 | tf_op jit(solution)/shard_map/ppermute | solution.py:27
  70.3 0.4 collective-permute-start.16
  70.7 22.1 %all-to-all-done.1 = bf16[32,144,128]{2,1,0:T(8,128)(2,1)S(1)} async-done(((bf16[32,144,128]{2,1,0:T(8,128)(2,1)}), bf16[32,144,128]{2,1,0:T(8,128)(2,1)S(1)}, u32[]{:S(2)}, u32[]{:S(2)}) %all-to-all-start.1) | async-done | bytes 1179680 | tf_op jit(solution)/shard_map/all_to_all | solution.py:36
  93.0 3.2 %convolution_convert_fusion.3 = bf16[128,416]{0,1:T(8,128)(2,1)S(1)} fusion(bf16[4096,416]{0,1:T(8,128)(2,1)} %param.22, bf16[4096,128]{1,0:T(8,128)(2,1)S(1)} %bitcast.124), kind=kOutput, calls=%fused_computation.8 | convolution fusion | flops 436260864 | bytes 4562944 | tf_op jit(solution)/shard_map/dot_general | solution.py:152
  96.2 1.1 convolution_convert_fusion.1
  97.3 3.0 %convolution_convert_fusion = bf16[128,416]{0,1:T(8,128)(2,1)S(1)} fusion(bf16[416,4096]{1,0:T(8,128)(2,1)} %collective-permute-done.9, bf16[4096,128]{1,0:T(8,128)(2,1)S(1)} %bitcast.126), kind=kOutput, calls=%fused_computation.5 | convolution fusion | flops 436260864 | bytes 4562944 | tf_op jit(solution)/shard_map/dot_general | solution.py:152
  100.3 3.0 %convolution_convert_fusion.2 = bf16[128,416]{0,1:T(8,128)(2,1)S(1)} fusion(bf16[416,4096]{1,0:T(8,128)(2,1)} %collective-permute-done.8, bf16[4096,128]{1,0:T(8,128)(2,1)S(1)} %bitcast.127), kind=kOutput, calls=%fused_computation.7 | convolution fusion | flops 436260864 | bytes 4562944 | tf_op jit(solution)/shard_map/dot_general | solution.py:152
  103.5 2.6 %collective-permute-start.12 = (bf16[432,128]{1,0:T(8,128)(2,1)S(1)}, bf16[432,128]{1,0:T(8,128)(2,1)S(1)}, u32[]{:S(2)}, u32[]{:S(2)}) collective-permute-start(bf16[432,128]{1,0:T(8,128)(2,1)S(1)} %get-tuple-element.16), channel_id=1, source_target_pairs={{0,3},{1,0},{2,1},{3,2},{4,7},{5,4},{6,5},{7,6},{8,11},{9,8},{10,9... | collective-permute-start | bytes 331784 | tf_op jit(solution)/shard_map/ppermute | solution.py:31
  106.2 0.6 collective-permute-start.11
  106.7 1.6 collective-permute-done.10
  108.3 3.0 %collective-permute-done.11 = bf16[432,128]{1,0:T(8,128)(2,1)S(1)} collective-permute-done((bf16[432,128]{1,0:T(8,128)(2,1)S(1)}, bf16[432,128]{1,0:T(8,128)(2,1)S(1)}, u32[]{:S(2)}, u32[]{:S(2)}) %collective-permute-start.11) | collective-permute-done | bytes 110624 | tf_op jit(solution)/shard_map/ppermute | solution.py:31
  111.4 0.7 collective-permute-start.14
  112.0 0.9 collective-permute-start.13
  112.9 1.8 %collective-permute-start.15 = (bf16[208,128]{1,0:T(8,128)(2,1)S(1)}, bf16[208,128]{1,0:T(8,128)(2,1)S(1)}, u32[]{:S(2)}, u32[]{:S(2)}) collective-permute-start(bf16[208,128]{1,0:T(8,128)(2,1)S(1)} %fusion.11), channel_id=1, source_target_pairs={{0,3},{1,0},{2,1},{3,2},{4,7},{5,4},{6,5},{7,6},{8,11},{9,8},{10,9... | collective-permute-start | bytes 159752 | tf_op jit(solution)/shard_map/ppermute | solution.py:31
  114.8 1.6 collective-permute-done.14
  116.4 0.3 collective-permute-done.13
  116.7 0.4 collective-permute-done.15
  117.1 2.7 %fusion.12 = f32[128,4096]{1,0:T(8,128)S(1)} fusion(bf16[416,4096]{1,0:T(8,128)(2,1)} %param.24, bf16[208,128]{1,0:T(8,128)(2,1)S(1)} %get-tuple-element.20, bf16[208,128]{1,0:T(8,128)(2,1)S(1)} %get-tuple-element.21), kind=kOutput, calls=%fused_computation.38 | convolution fusion | flops 436420608 | bytes 5611520 | tf_op jit(solution)/shard_map/dot_general | solution.py:186
  119.8 2.7 %fusion.1 = bf16[16,32,8,128]{3,2,1,0:T(8,128)(2,1)S(1)} fusion(f32[128,4096]{1,0:T(8,128)S(1)} %fusion.12, bf16[416,4096]{1,0:T(8,128)(2,1)} %collective-permute-done.16, bf16[208,128]{1,0:T(8,128)(2,1)S(1)} %get-tuple-element.19, bf16[208,128]{1,0:T(8,128)(2,1)S(1)} %get-tuple-element.18), kind=kOutput, calls=%fused_computation.4 | convolution fusion | flops 437469184 | bytes 6660096 | tf_op jit(solution)/shard_map/dot_general | solution.py:186
  122.5 1.3 copy.45
  123.8 7.7 %all-to-all-start.2 = ((bf16[32,128,128]{1,2,0:T(8,128)(2,1)}), bf16[32,128,128]{1,2,0:T(8,128)(2,1)S(1)}, u32[]{:S(2)}, u32[]{:S(2)}) async-start(bf16[32,128,128]{1,2,0:T(8,128)(2,1)} %bitcast.122), calls=%async_computation.2 | async-start | bytes 2097152 | tf_op jit(solution)/shard_map/all_to_all | solution.py:36
  131.5 19.4 %all-to-all-done.2 = bf16[32,128,128]{1,2,0:T(8,128)(2,1)S(1)} async-done(((bf16[32,128,128]{1,2,0:T(8,128)(2,1)}), bf16[32,128,128]{1,2,0:T(8,128)(2,1)S(1)}, u32[]{:S(2)}, u32[]{:S(2)}) %all-to-all-start.2) | async-done | bytes 1048608 | tf_op jit(solution)/shard_map/all_to_all | solution.py:36
  151.2 9.4 %collective-permute-start.17 = (bf16[64,128]{1,0:T(8,128)(2,1)S(1)}, bf16[64,128]{1,0:T(8,128)(2,1)S(1)}, u32[]{:S(2)}, u32[]{:S(2)}) collective-permute-start(bf16[64,128]{1,0:T(8,128)(2,1)S(1)} %get-tuple-element.26), channel_id=1, source_target_pairs={{0,4},{4,0},{8,12},{12,8},{16,20},{20,16},{24,28},{28,24},{32,36},... | collective-permute-start | bytes 49160 | tf_op jit(solution)/shard_map/ppermute | solution.py:27
  160.6 0.8 collective-permute-done.17
  161.5 0.8 fusion.5
  (72 shorter events, 1.8 us)
Async XLA Ops:
  0.0 7.9 %copy-start = (bf16[4,2,256,128]{3,2,1,0:T(8,128)(2,1)S(1)}, bf16[4,2,256,128]{3,2,1,0:T(8,128)(2,1)}, u32[]{:S(2)}) copy-start(bf16[4,2,256,128]{3,2,1,0:T(8,128)(2,1)} %param.14) | copy-start | bytes 1572868
  0.0 7.7 %copy-start.9 = (s32[4]{0:T(128)S(1)}, s32[4]{0:T(128)}, u32[]{:S(2)}) copy-start(s32[4]{0:T(128)} %param.18) | copy-start | bytes 52
  0.0 7.8 %copy-start.4 = (bf16[4,256]{1,0:T(4,128)(2,1)S(1)}, bf16[4,256]{1,0:T(4,128)(2,1)}, u32[]{:S(2)}) copy-start(bf16[4,256]{1,0:T(4,128)(2,1)} %param.16) | copy-start | bytes 6148
  0.0 7.8 %copy-start.2 = (bf16[4,4096]{1,0:T(4,128)(2,1)S(1)}, bf16[4,4096]{1,0:T(4,128)(2,1)}, u32[]{:S(2)}) copy-start(bf16[4,4096]{1,0:T(4,128)(2,1)} %param.13) | copy-start | bytes 98308
  0.0 8.5 %copy-start.5 = (bf16[4,256]{1,0:T(4,128)(2,1)S(1)}, bf16[4,256]{1,0:T(4,128)(2,1)}, u32[]{:S(2)}) copy-start(bf16[4,256]{1,0:T(4,128)(2,1)} %param.17) | copy-start | bytes 6148
  0.0 8.5 %copy-start.8 = (bf16[4,2,256,128]{3,2,1,0:T(8,128)(2,1)S(1)}, bf16[4,2,256,128]{3,2,1,0:T(8,128)(2,1)}, u32[]{:S(2)}) copy-start(bf16[4,2,256,128]{3,2,1,0:T(8,128)(2,1)} %param.15) | copy-start | bytes 1572868
  2.7 19.0 %collective-permute-start.1 = (bf16[64,4096]{1,0:T(8,128)(2,1)}, bf16[64,4096]{1,0:T(8,128)(2,1)}, u32[]{:S(2)}, u32[]{:S(2)}) collective-permute-start(bf16[64,4096]{1,0:T(8,128)(2,1)} %get-tuple-element.10), channel_id=1, source_target_pairs={{0,1},{1,2},{2,3},{3,0},{4,5},{5,6},{6,7},{7,4},{8,9},{9,10},{10,1... | collective-permute-start | bytes 1572872 | tf_op jit(solution)/shard_map/ppermute | solution.py:31
  4.7 17.0 %collective-permute-start.3 = (bf16[64,4096]{1,0:T(8,128)(2,1)S(1)}, bf16[64,4096]{1,0:T(8,128)(2,1)}, u32[]{:S(2)}, u32[]{:S(2)}) collective-permute-start(bf16[64,4096]{1,0:T(8,128)(2,1)S(1)} %get-tuple-element.11), channel_id=1, source_target_pairs={{0,3},{1,0},{2,1},{3,2},{4,7},{5,4},{6,5},{7,6},{8,11},{9,8},{10,9... | collective-permute-start | bytes 1572872 | tf_op jit(solution)/shard_map/ppermute | solution.py:31
  6.0 24.1 %collective-permute-start.2 = (bf16[64,4096]{1,0:T(8,128)(2,1)S(1)}, bf16[64,4096]{1,0:T(8,128)(2,1)}, u32[]{:S(2)}, u32[]{:S(2)}) collective-permute-start(bf16[64,4096]{1,0:T(8,128)(2,1)S(1)} %get-tuple-element.12), channel_id=1, source_target_pairs={{0,2},{1,3},{2,0},{3,1},{4,6},{5,7},{6,4},{7,5},{8,10},{9,11},{10,... | collective-permute-start | bytes 1572872 | tf_op jit(solution)/shard_map/ppermute | solution.py:31
  10.3 24.2 %copy-start.1 = (bf16[256,256]{1,0:T(8,128)(2,1)S(1)}, bf16[256,256]{1,0:T(8,128)(2,1)}, u32[]{:S(2)}) copy-start(bf16[256,256]{1,0:T(8,128)(2,1)} %constant.164.clone) | copy-start | bytes 393220
  10.3 24.2 %copy-start.3 = (bf16[256,64]{0,1:T(8,128)(2,1)S(1)}, bf16[256,64]{0,1:T(8,128)(2,1)}, u32[]{:S(2)}) copy-start(bf16[256,64]{0,1:T(8,128)(2,1)} %param.19) | copy-start | bytes 98308
  10.3 24.4 %copy-start.6 = (bf16[64]{0:T(256)(128)(2,1)S(1)}, bf16[64]{0:T(256)(128)(2,1)}, u32[]{:S(2)}) copy-start(bf16[64]{0:T(256)(128)(2,1)} %param.21) | copy-start | bytes 388
  10.3 35.8 %all-to-all-start = ((bf16[32,4,4096]{2,1,0:T(4,128)(2,1)}), bf16[32,4,4096]{2,1,0:T(4,128)(2,1)S(1)}, u32[]{:S(2)}, u32[]{:S(2)}) async-start(bf16[32,4,4096]{2,1,0:T(4,128)(2,1)} %broadcast_in_dim.26), calls=%async_computation | async-start | bytes 2097152 | tf_op jit(solution)/shard_map/all_to_all | solution.py:36
  33.0 15.8 %collective-permute-start.4 = (bf16[256,4096]{1,0:T(8,128)(2,1)}, bf16[256,4096]{1,0:T(8,128)(2,1)}, u32[]{:S(2)}, u32[]{:S(2)}) collective-permute-start(bf16[256,4096]{1,0:T(8,128)(2,1)} %pad_maximum_fusion), channel_id=1, source_target_pairs={{0,4},{4,0},{8,12},{12,8},{16,20},{20,16},{24,28},{28,24},{32,36},... | collective-permute-start | bytes 6291464 | tf_op jit(solution)/shard_map/ppermute | solution.py:27
  34.8 19.3 %collective-permute-start = (bf16[64,256]{1,0:T(8,128)(2,1)S(1)}, bf16[64,256]{1,0:T(8,128)(2,1)S(1)}, u32[]{:S(2)}, u32[]{:S(2)}) collective-permute-start(bf16[64,256]{1,0:T(8,128)(2,1)S(1)} %pad_maximum_fusion.4), channel_id=1, source_target_pairs={{0,4},{4,0},{8,12},{12,8},{16,20},{20,16},{24,28},{28,24},{32,36},... | collective-permute-start | bytes 98312 | tf_op jit(solution)/shard_map/ppermute | solution.py:27
  51.1 3.0 %collective-permute-start.5 = (bf16[128,128]{1,0:T(8,128)(2,1)S(1)}, bf16[128,128]{1,0:T(8,128)(2,1)S(1)}, u32[]{:S(2)}, u32[]{:S(2)}) collective-permute-start(bf16[128,128]{1,0:T(8,128)(2,1)S(1)} %get-tuple-element.22), channel_id=1, source_target_pairs={{0,3},{1,0},{2,1},{3,2},{4,7},{5,4},{6,5},{7,6},{8,11},{9,8},{10,9... | collective-permute-start | bytes 98312 | tf_op jit(solution)/shard_map/ppermute | solution.py:31
  52.0 4.0 %collective-permute-start.7 = (bf16[128,128]{1,0:T(8,128)(2,1)S(1)}, bf16[128,128]{1,0:T(8,128)(2,1)S(1)}, u32[]{:S(2)}, u32[]{:S(2)}) collective-permute-start(bf16[128,128]{1,0:T(8,128)(2,1)S(1)} %get-tuple-element.23), channel_id=1, source_target_pairs={{0,1},{1,2},{2,3},{3,0},{4,5},{5,6},{6,7},{7,4},{8,9},{9,10},{10,1... | collective-permute-start | bytes 98312 | tf_op jit(solution)/shard_map/ppermute | solution.py:31
  52.6 4.3 %collective-permute-start.6 = (bf16[128,128]{1,0:T(8,128)(2,1)S(1)}, bf16[128,128]{1,0:T(8,128)(2,1)S(1)}, u32[]{:S(2)}, u32[]{:S(2)}) collective-permute-start(bf16[128,128]{1,0:T(8,128)(2,1)S(1)} %get-tuple-element.24), channel_id=1, source_target_pairs={{0,2},{1,3},{2,0},{3,1},{4,6},{5,7},{6,4},{7,5},{8,10},{9,11},{10,... | collective-permute-start | bytes 98312 | tf_op jit(solution)/shard_map/ppermute | solution.py:31
  58.2 34.6 %all-to-all-start.1 = ((bf16[32,144,128]{2,1,0:T(8,128)(2,1)}), bf16[32,144,128]{2,1,0:T(8,128)(2,1)S(1)}, u32[]{:S(2)}, u32[]{:S(2)}) async-start(bf16[32,144,128]{2,1,0:T(8,128)(2,1)} %broadcast_in_dim.27), calls=%async_computation.1 | async-start | bytes 2359296 | tf_op jit(solution)/shard_map/all_to_all | solution.py:36
  67.0 30.3 %collective-permute-start.9 = (bf16[416,4096]{1,0:T(8,128)(2,1)}, bf16[416,4096]{1,0:T(8,128)(2,1)}, u32[]{:S(2)}, u32[]{:S(2)}) collective-permute-start(bf16[416,4096]{1,0:T(8,128)(2,1)} %bitcast.142), channel_id=1, source_target_pairs={{0,4},{4,0},{8,12},{12,8},{16,20},{20,16},{24,28},{28,24},{32,36},... | collective-permute-start | bytes 10223624 | tf_op jit(solution)/shard_map/ppermute | solution.py:27
  70.2 30.1 %collective-permute-start.8 = (bf16[416,4096]{1,0:T(8,128)(2,1)}, bf16[416,4096]{1,0:T(8,128)(2,1)}, u32[]{:S(2)}, u32[]{:S(2)}) collective-permute-start(bf16[416,4096]{1,0:T(8,128)(2,1)} %bitcast.143), channel_id=1, source_target_pairs={{0,4},{4,0},{8,12},{12,8},{16,20},{20,16},{24,28},{28,24},{32,36},... | collective-permute-start | bytes 10223624 | tf_op jit(solution)/shard_map/ppermute | solution.py:27
  70.3 49.5 %collective-permute-start.16 = (bf16[416,4096]{1,0:T(8,128)(2,1)}, bf16[416,4096]{1,0:T(8,128)(2,1)}, u32[]{:S(2)}, u32[]{:S(2)}) collective-permute-start(bf16[416,4096]{1,0:T(8,128)(2,1)} %param.24), channel_id=1, source_target_pairs={{0,4},{4,0},{8,12},{12,8},{16,20},{20,16},{24,28},{28,24},{32,36},... | collective-permute-start | bytes 10223624 | tf_op jit(solution)/shard_map/ppermute | solution.py:27
  92.9 3.3 %copy-start.7 = (bf16[4096,416]{0,1:T(8,128)(2,1)S(1)}, bf16[4096,416]{0,1:T(8,128)(2,1)}, u32[]{:S(2)}) copy-start(bf16[4096,416]{0,1:T(8,128)(2,1)} %param.23) | copy-start | bytes 10223620
  103.4 4.9 %collective-permute-start.10 = (bf16[432,128]{1,0:T(8,128)(2,1)S(1)}, bf16[432,128]{1,0:T(8,128)(2,1)S(1)}, u32[]{:S(2)}, u32[]{:S(2)}) collective-permute-start(bf16[432,128]{1,0:T(8,128)(2,1)S(1)} %get-tuple-element.15), channel_id=1, source_target_pairs={{0,1},{1,2},{2,3},{3,0},{4,5},{5,6},{6,7},{7,4},{8,9},{9,10},{10,1... | collective-permute-start | bytes 331784 | tf_op jit(solution)/shard_map/ppermute | solution.py:31
  103.5 4.8 %collective-permute-start.12 = (bf16[432,128]{1,0:T(8,128)(2,1)S(1)}, bf16[432,128]{1,0:T(8,128)(2,1)S(1)}, u32[]{:S(2)}, u32[]{:S(2)}) collective-permute-start(bf16[432,128]{1,0:T(8,128)(2,1)S(1)} %get-tuple-element.16), channel_id=1, source_target_pairs={{0,3},{1,0},{2,1},{3,2},{4,7},{5,4},{6,5},{7,6},{8,11},{9,8},{10,9... | collective-permute-start | bytes 331784 | tf_op jit(solution)/shard_map/ppermute | solution.py:31
  106.2 5.1 %collective-permute-start.11 = (bf16[432,128]{1,0:T(8,128)(2,1)S(1)}, bf16[432,128]{1,0:T(8,128)(2,1)S(1)}, u32[]{:S(2)}, u32[]{:S(2)}) collective-permute-start(bf16[432,128]{1,0:T(8,128)(2,1)S(1)} %get-tuple-element.17), channel_id=1, source_target_pairs={{0,2},{1,3},{2,0},{3,1},{4,6},{5,7},{6,4},{7,5},{8,10},{9,11},{10,... | collective-permute-start | bytes 331784 | tf_op jit(solution)/shard_map/ppermute | solution.py:31
  111.4 5.0 %collective-permute-start.14 = (bf16[208,128]{1,0:T(8,128)(2,1)S(1)}, bf16[208,128]{1,0:T(8,128)(2,1)S(1)}, u32[]{:S(2)}, u32[]{:S(2)}) collective-permute-start(bf16[208,128]{1,0:T(8,128)(2,1)S(1)} %fusion.11), channel_id=1, source_target_pairs={{0,2},{1,3},{2,0},{3,1},{4,6},{5,7},{6,4},{7,5},{8,10},{9,11},{10,... | collective-permute-start | bytes 159752 | tf_op jit(solution)/shard_map/ppermute | solution.py:31
  112.0 4.6 %collective-permute-start.13 = (bf16[208,128]{1,0:T(8,128)(2,1)S(1)}, bf16[208,128]{1,0:T(8,128)(2,1)S(1)}, u32[]{:S(2)}, u32[]{:S(2)}) collective-permute-start(bf16[208,128]{1,0:T(8,128)(2,1)S(1)} %fusion.11), channel_id=1, source_target_pairs={{0,1},{1,2},{2,3},{3,0},{4,5},{5,6},{6,7},{7,4},{8,9},{9,10},{10,1... | collective-permute-start | bytes 159752 | tf_op jit(solution)/shard_map/ppermute | solution.py:31
  112.9 4.1 %collective-permute-start.15 = (bf16[208,128]{1,0:T(8,128)(2,1)S(1)}, bf16[208,128]{1,0:T(8,128)(2,1)S(1)}, u32[]{:S(2)}, u32[]{:S(2)}) collective-permute-start(bf16[208,128]{1,0:T(8,128)(2,1)S(1)} %fusion.11), channel_id=1, source_target_pairs={{0,3},{1,0},{2,1},{3,2},{4,7},{5,4},{6,5},{7,6},{8,11},{9,8},{10,9... | collective-permute-start | bytes 159752 | tf_op jit(solution)/shard_map/ppermute | solution.py:31
  123.8 27.1 %all-to-all-start.2 = ((bf16[32,128,128]{1,2,0:T(8,128)(2,1)}), bf16[32,128,128]{1,2,0:T(8,128)(2,1)S(1)}, u32[]{:S(2)}, u32[]{:S(2)}) async-start(bf16[32,128,128]{1,2,0:T(8,128)(2,1)} %bitcast.122), calls=%async_computation.2 | async-start | bytes 2097152 | tf_op jit(solution)/shard_map/all_to_all | solution.py:36
  151.2 10.2 %collective-permute-start.17 = (bf16[64,128]{1,0:T(8,128)(2,1)S(1)}, bf16[64,128]{1,0:T(8,128)(2,1)S(1)}, u32[]{:S(2)}, u32[]{:S(2)}) collective-permute-start(bf16[64,128]{1,0:T(8,128)(2,1)S(1)} %get-tuple-element.26), channel_id=1, source_target_pairs={{0,4},{4,0},{8,12},{12,8},{16,20},{20,16},{24,28},{28,24},{32,36},... | collective-permute-start | bytes 49160 | tf_op jit(solution)/shard_map/ppermute | solution.py:27

commit v2 on v1

--- a/solution.py
+++ b/solution.py
@@ -2,6 +2,8 @@
 import jax.numpy as jnp
 import numpy as np
 from jax import lax
+from jax.experimental import pallas as pl
+from jax.experimental.pallas import tpu as pltpu
 from jax.sharding import PartitionSpec as P
 
 D = 16384
@@ -9,6 +11,10 @@
 CORES = 2
 QUARTERS = 4
 ROWS_HERE = 4
+HALF = PLANE * ROWS_HERE
+PAIR = 128
+PARTS = 2
+TAIL = 16
 
 F32 = jnp.float32
 BF16 = jnp.bfloat16
@@ -68,6 +74,176 @@
     weighted_value_sum = weighted_value_sum + new_low[..., None] * fresh_values[:, :, None, :]
     attended = (weighted_value_sum / denominator[..., None]).astype(BF16)
     return attended.reshape(row_count, kv_heads * group_size * head_size)
+
+
+VMEM = pl.BlockSpec(memory_space=pltpu.VMEM)
+SMEM = pl.BlockSpec(memory_space=pltpu.SMEM)
+HBM = pl.BlockSpec(memory_space=pltpu.HBM)
+
+
+def kernel_call(body, outs, scratch=(), scalars=1, streamed=0, inputs=0, limit=8):
+    return pl.pallas_call(
+        body,
+        out_shape=outs,
+        in_specs=[SMEM] * scalars + [HBM] * streamed + [VMEM] * inputs,
+        out_specs=[VMEM] * len(outs),
+        scratch_shapes=list(scratch),
+        compiler_params=pltpu.CompilerParams(vmem_limit_bytes=limit * 2**20),
+    )
+
+
+def held(value):
+    return pltpu.with_memory_space_constraint(value, pltpu.VMEM)
+
+
+def halves(source, target, sems):
+    rows = source.shape[0] // PARTS
+    return [
+        pltpu.make_async_copy(
+            source.at[pl.ds(part * rows, rows)], target.at[pl.ds(part * rows, rows)], sems.at[part]
+        )
+        for part in range(PARTS)
+    ]
+
+
+def run_copies(copies):
+    for copy in copies:
+        copy.start()
+    for copy in copies:
+        copy.wait()
+
+
+def cut_kernel(place_ref, weights_ref, *refs):
+    outs, sems = refs[:-1], refs[-1]
+    width = outs[0].shape[1]
+    copies = []
+    for step, out in enumerate(outs, 1):
+        start = pl.multiple_of(lax.rem(place_ref[0] + step, QUARTERS) * width, width)
+        copies.append(
+            pltpu.make_async_copy(
+                weights_ref.at[:, pl.ds(start, width)], out, sems.at[step - 1]
+            )
+        )
+    run_copies(copies)
+
+
+def cut(place, weights, width):
+    piece = jax.ShapeDtypeStruct((weights.shape[0], width), weights.dtype)
+    return pl.pallas_call(
+        cut_kernel,
+        out_shape=[piece] * (QUARTERS - 1),
+        in_specs=[SMEM, HBM],
+        out_specs=[VMEM] * (QUARTERS - 1),
+        scratch_shapes=[pltpu.SemaphoreType.DMA((QUARTERS - 1,))],
+    )(place, in_hbm(weights))
+
+
+def in_hbm(value):
+    return pltpu.with_memory_space_constraint(value, pltpu.HBM)
+
+
+def load_kernel(*refs):
+    count, sems = len(refs) // 2, refs[-1]
+    run_copies(
+        [
+            copy
+            for place in range(count)
+            for copy in halves(refs[place], refs[count + place], sems.at[place])
+        ]
+    )
+
+
+def loaded(*values):
+    return pl.pallas_call(
+        load_kernel,
+        out_shape=[pltpu.VMEM(v.shape, v.dtype) for v in values],
+        in_specs=[HBM] * len(values),
+        out_specs=[VMEM] * len(values),
+        scratch_shapes=[pltpu.SemaphoreType.DMA((len(values), PARTS))],
+        compiler_params=pltpu.CompilerParams(vmem_limit_bytes=2 * 2**20),
+    )(*[in_hbm(v) for v in values])
+
+
+def spread(squares):
+    high = squares.astype(BF16)
+    low = (squares - high.astype(F32)).astype(BF16)
+    row = lax.broadcasted_iota(jnp.int32, (TAIL, squares.shape[1]), 0)
+    high, low = high.astype(F32), low.astype(F32)
+    return jnp.where(row == 0, high, jnp.where(row == 1, low, 0.0)).astype(BF16)
+
+
+def hsum_kernel(own_ref, a_ref, b_ref, c_ref, residual_ref, gain_ref, hsum_ref, blocks_ref):
+    hsum = (
+        residual_ref[...].astype(F32)
+        + own_ref[...]
+        + a_ref[...].astype(F32)
+        + b_ref[...].astype(F32)
+        + c_ref[...].astype(F32)
+    )
+    hsum_ref[...] = hsum
+    scaled = (hsum * gain_ref[...].astype(F32)).astype(BF16)
+    tail = spread(jnp.sum(hsum * hsum, axis=0, keepdims=True))
+    for p in range(PLANE):
+        blocks_ref[p, :PAIR, :] = scaled
+        blocks_ref[p, PAIR:, :] = tail
+
+
+def expand_kernel(a_step, b_step, c_step, d_step, *refs):
+    weights, blocks_ref, outs = refs[:4], refs[4], refs[5 : 5 + QUARTERS]
+    features, sums, buffer, sems = refs[5 + QUARTERS :]
+    copies = [
+        halves(ref, buffer.at[place], sems.at[place]) for place, ref in enumerate(weights)
+    ]
+    for group in copies:
+        for copy in group:
+            copy.start()
+    steps = [ref[0] for ref in (a_step, b_step, c_step, d_step)]
+    units = weights[0].shape[0] // 2
+    squares = jnp.zeros((TAIL, HALF), F32)
+    for p in range(PLANE):
+        features[p * PAIR : (p + 1) * PAIR, :] = blocks_ref[p, :PAIR, :]
+        squares = squares + blocks_ref[p, PAIR:, :].astype(F32)
+    tail = spread(squares[0:1] + squares[1:2])
+    for place, group in enumerate(copies):
+        for copy in group:
+            copy.wait()
+        sums[place * 2 * units : (place + 1) * 2 * units, :] = jnp.dot(
+            buffer[place], features[...], preferred_element_type=F32
+        )
+    for part in range(QUARTERS):
+        start = (part // 2 * 4 + part % 2) * units
+        gates, ups = slice(start, start + units), slice(start + 2 * units, start + 3 * units)
+        for step in range(QUARTERS):
+
+            @pl.when(steps[part] == step)
+            def _(gates=gates, ups=ups, step=step):
+                outs[step][:units, :] = sums[gates, :].astype(BF16)
+                outs[step][units : 2 * units, :] = sums[ups, :].astype(BF16)
+                outs[step][2 * units :, :] = tail
+
+
+def hidden_kernel(a_ref, b_ref, c_ref, d_ref, hidden_ref):
+    units = hidden_ref.shape[0]
+    total = a_ref[...].astype(F32) + b_ref[...].astype(F32)
+    total = total + c_ref[...].astype(F32) + d_ref[...].astype(F32)
+    squares = total[2 * units : 2 * units + 1] + total[2 * units + 1 : 2 * units + 2]
+    inverse = lax.rsqrt(squares / D + 1e-05)
+    gate = total[:units] * inverse
+    up = total[units : 2 * units] * inverse
+    hidden_ref[...] = (gate / (1.0 + jnp.exp(-gate)) * up).astype(BF16)
+
+
+def contract_kernel(places_ref, own_ref, other_ref, a_ref, b_ref, c_ref, d_ref, out_ref, hidden):
+    for step, ref in enumerate((a_ref, b_ref, c_ref, d_ref)):
+        start = pl.multiple_of(places_ref[step] * ref.shape[0], 16)
+        hidden[pl.ds(start, ref.shape[0]), :] = ref[...]
+    values = hidden[...].astype(F32).T.astype(BF16)
+    for p in range(0, PLANE, 2):
+        columns = slice(p * PAIR, (p + 2) * PAIR)
+        rows = jnp.concatenate([own_ref[:, columns], other_ref[:, columns]], 0)
+        part = jnp.dot(values, rows, preferred_element_type=F32).astype(BF16)
+        out_ref[p] = part[:, :PAIR]
+        out_ref[p + 1] = part[:, PAIR:]
 
 
 def pair_order(own, other, core):
@@ -99,9 +275,8 @@
 
     out_rows = out_weight.T
     own_out = [lax.dynamic_slice_in_dim(out_rows, quarter * width, width, 1)]
-    for step in range(1, QUARTERS):
-        to = (quarter + step) % QUARTERS
-        own_out.append(along_gy(lax.dynamic_slice_in_dim(out_rows, to * width, width, 1), step))
+    pieces = cut(quarter.astype(jnp.int32).reshape(1), out_rows, width)
+    own_out += [along_gy(piece, step) for step, piece in enumerate(pieces, 1)]
     own_out = jnp.concatenate(own_out, 0)
 
     gate_other, up_other = to_core(gate_weight.T), to_core(up_weight.T)
@@ -112,8 +287,8 @@
     mine = lax.dynamic_slice_in_dim(residual, core * half, half, 1)
     theirs = lax.dynamic_slice_in_dim(residual, (1 - core) * half, half, 1)
     received = to_core(jnp.concatenate([theirs, gain], 1))
-    residual = pair_order(mine, received[:, :half], core).astype(F32)
-    gain = pair_order(gain, received[:, half:], core).astype(F32)
+    residual = pair_order(mine, received[:, :half], core)
+    gain = pair_order(gain, received[:, half:], core)
 
     attended = attend(query, key_cache, value_cache, key_new, value_new, lengths)
     gathered = plane_exchange(jnp.broadcast_to(attended[None], (PLANE,) + attended.shape))
@@ -132,66 +307,63 @@
         jnp.concatenate([own_part, other_part], 1),
         jnp.concatenate([other_part, own_part], 1),
     )
-    projected = parts[0]
-    for step in range(1, QUARTERS):
-        projected = projected + along_gy(parts[step].astype(BF16), -step).astype(F32)
-    hsum = residual + projected
-
-    squares = jnp.sum(hsum * hsum, axis=0, keepdims=True)
-    high = squares.astype(BF16)
-    low = (squares - high.astype(F32)).astype(BF16)
-    block = jnp.concatenate(
-        [(hsum * gain).astype(BF16), high, low, jnp.zeros((14, half), BF16)], 0
-    )
-    blocks = plane_exchange(jnp.broadcast_to(block[None], (PLANE,) + block.shape))
-    features = blocks[:, : CORES * columns].reshape(width, half)
-    squares = jnp.sum(blocks[:, 128].astype(F32) + blocks[:, 129].astype(F32), axis=0)
-
+    sums = [parts[0]] + [
+        along_gy(parts[step].astype(BF16), -step) for step in range(1, QUARTERS)
+    ]
+    hsum, blocks = kernel_call(
+        hsum_kernel,
+        [
+            jax.ShapeDtypeStruct((PAIR, HALF), F32),
+            jax.ShapeDtypeStruct((PLANE, PAIR + TAIL, HALF), BF16),
+        ],
+        scalars=0,
+        inputs=6,
+    )(*sums, residual, gain)
+
+    steps = [
+        ((((part // 2) ^ core) * 2 + part % 2 - quarter) % QUARTERS).reshape(1)
+        for part in range(QUARTERS)
+    ]
+    blocks = plane_exchange(blocks)
     units = gate_weight.shape[1] // 2
-    def expand(weights):
-        return jnp.dot(weights, features, preferred_element_type=F32).reshape(2, units, half)
-
-    gates = jnp.concatenate([expand(gate_weight.T), expand(gate_other)], 0)
-    ups = jnp.concatenate([expand(up_weight.T), expand(up_other)], 0)
-    high = squares.astype(BF16)
-    low = (squares - high.astype(F32)).astype(BF16)
-    tail = jnp.concatenate([high[None], low[None], jnp.zeros((14, half), BF16)], 0)
-    tail = jnp.broadcast_to(tail[None], (QUARTERS,) + tail.shape)
-    sends = jnp.concatenate([gates.astype(BF16), ups.astype(BF16), tail], 1)
-
-    def chunk_of(to):
-        return ((to // 2) ^ core) * 2 + to % 2
-
-    total = lax.dynamic_index_in_dim(sends, chunk_of(quarter), 0, False).astype(F32)
-    for step in range(1, QUARTERS):
-        to = (quarter + step) % QUARTERS
-        part = lax.dynamic_index_in_dim(sends, chunk_of(to), 0, False)
-        total = total + along_gy(part, step).astype(F32)
-    squares = total[2 * units : 2 * units + 1] + total[2 * units + 1 : 2 * units + 2]
-    inverse = lax.rsqrt(squares / D + 1e-05)
-    gate = total[:units] * inverse
-    up = total[units : 2 * units] * inverse
-    hidden = (jax.nn.silu(gate) * up).astype(BF16)
-
-    chunks = jnp.stack([hidden] + [along_gy(hidden, step) for step in range(1, QUARTERS)])
-    ordered = [
-        lax.dynamic_index_in_dim(
-            chunks, (quarter - (((place // 2) ^ core) * 2 + place % 2)) % QUARTERS, 0, False
-        )
-        for place in range(QUARTERS)
-    ]
-    hidden = jnp.concatenate(ordered, 0)
-
-    def contract(weights, values):
-        return lax.dot_general(
-            weights, values, (((0,), (0,)), ((), ())), preferred_element_type=F32
-        )
-
-    branch = contract(down_weight, hidden[: 2 * units]) + contract(down_other, hidden[2 * units :])
-    branch = branch.astype(BF16).reshape(PLANE, CORES * columns, half)
+    message = jax.ShapeDtypeStruct((2 * units + TAIL, HALF), BF16)
+    sends = kernel_call(
+        expand_kernel,
+        [message] * QUARTERS,
+        scratch=[
+            pltpu.VMEM((width, HALF), BF16),
+            pltpu.VMEM((8 * units, HALF), F32),
+            pltpu.VMEM((4, 2 * units, width), BF16),
+            pltpu.SemaphoreType.DMA((4, PARTS)),
+        ],
+        scalars=QUARTERS,
+        streamed=4,
+        inputs=1,
+        limit=22,
+    )(
+        *steps,
+        in_hbm(gate_weight.T),
+        in_hbm(up_weight.T),
+        in_hbm(gate_other),
+        in_hbm(up_other),
+        held(blocks),
+    )
+    sends = [sends[0]] + [along_gy(sends[step], step) for step in range(1, QUARTERS)]
+    (hidden,) = kernel_call(
+        hidden_kernel, [jax.ShapeDtypeStruct((units, HALF), BF16)], scalars=0, inputs=4
+    )(*sends)
+    chunks = [hidden] + [along_gy(hidden, step) for step in range(1, QUARTERS)]
+    source = (quarter - jnp.arange(QUARTERS, dtype=jnp.int32)) % QUARTERS
+    places = ((source // 2) ^ core) * 2 + source % 2
+    (branch,) = kernel_call(
+        contract_kernel,
+        [jax.ShapeDtypeStruct((PLANE, HALF, PAIR), BF16)],
+        scratch=[pltpu.VMEM((4 * units, HALF), BF16)],
+        inputs=6,
+    )(places, *[held(w) for w in loaded(down_weight, down_other)], *chunks)
     branch = jnp.sum(plane_exchange(branch).astype(F32), axis=0)
 
-    out = (hsum + branch).astype(BF16)
+    out = (hsum + branch.T).astype(BF16)
     mine = lax.dynamic_slice_in_dim(out, core * columns, columns, 0)
     theirs = to_core(lax.dynamic_slice_in_dim(out, (1 - core) * columns, columns, 0))
     out = jnp.where(

time: 163 us -> 160 us (0.982)
  Pallas kernels: 0 us -> 19.4 us
  matrix products: 21.9 us -> 6.23 us
  local copies, waits for them, and re-layouts: 7.3 us -> 3.13 us
  starting transfers between devices: 57.2 us -> 55 us
  other arithmetic: 3.77 us -> 2 us
    pallas_call x0 -> x6, Pallas kernels: none -> 19.4 us  [the longest x1 9.73 us: per_device(): kernel_call(expand_kernel, [message] * QUARTERS, scratch=[pltpu.VMEM((wid...]
    dot_general x6 -> x0, matrix products: 15.7 us -> none  [the longest x4 10.2 us: expand(): jnp.dot(weights, features, preferred_element_type=F32)]
    ppermute x6, waiting for transfers between devices: 0.85 us -> 3.36 us  [to_core(): return lax.ppermute(value, 'gx', [(g, g ^ 1) for g in range(PLANE * CORES)])]
  transfers between devices with their start and end apart: 21 -> 21, of which waited for: 12 -> 14; matrix products, arithmetic and copies ran while one was open for 15% -> 6% of each run, Pallas kernels for 0% -> 9%
where the time goes in v2:
time: 160 us; the launch traced here: 159 us
  waiting for transfers between devices  72.9 us (46%)
  starting transfers between devices  55 us (34%)
  Pallas kernels  19.4 us (12%)
  matrix products  6.23 us (4%)
  local copies, waits for them, and re-layouts  3.13 us (2%)
  other arithmetic  2 us (1%)
    all_to_all x3, waiting for transfers between devices, plane_exchange(): lax.all_to_all(blocks, 'gx', 0, 0, axis_index_groups=groups, tiled=True)  51.7 us
    all_to_all x3, starting transfers between devices, plane_exchange(): lax.all_to_all(blocks, 'gx', 0, 0, axis_index_groups=groups, tiled=True)  27.1 us
    ppermute x12, waiting for transfers between devices, along_gy(): lax.ppermute(value, 'gy', [(i, (i + step) % QUARTERS) for i in range(QUAR...  17.9 us
    ppermute x6, starting transfers between devices, to_core(): return lax.ppermute(value, 'gx', [(g, g ^ 1) for g in range(PLANE * CORES)])  14 us
    ppermute x12, starting transfers between devices, along_gy(): lax.ppermute(value, 'gy', [(i, (i + step) % QUARTERS) for i in range(QUAR...  13.9 us
    pallas_call x1, Pallas kernels, per_device(): kernel_call(expand_kernel, [message] * QUARTERS, scratch=[pltpu.VMEM((wid...  9.73 us
    dot_general x2, matrix products, project(): lax.dot_general(weights, rows, (((1,), (1,)), ((), ())), preferred_elemen...  4.59 us
    ppermute x6, waiting for transfers between devices, to_core(): return lax.ppermute(value, 'gx', [(g, g ^ 1) for g in range(PLANE * CORES)])  3.36 us
  transfers between devices with their start and end apart: 21, of which 14 were waited for; matrix products, arithmetic and copies ran while one was open for 6% of the time, Pallas kernels for 9%

profile of v2, /device:TPU:1, one launch (start us, length us, event | category | flops | bytes accessed | tf_op | source)
XLA Modules:
  0.0 159.2 jit_solution(17404779714891772322)
XLA Ops:
  0.0 2.6 %shard_map.127 = (bf16[64,4096]{1,0:T(8,128)(2,1)}, bf16[64,4096]{1,0:T(8,128)(2,1)}, bf16[64,4096]{1,0:T(8,128)(2,1)}) custom-call(s32[1]{0:T(128)} %bitcast.1.place_ref, bf16[64,16384]{1,0:T(8,128)(2,1)} %bitcast.56), custom_call_target="tpu_custom_call" | custom-call | tf_op jit(solution)/shard_map/pallas_call | solution.py:132
  2.7 2.1 %collective-permute-start = (bf16[64,4096]{1,0:T(8,128)(2,1)}, bf16[64,4096]{1,0:T(8,128)(2,1)S(1)}, u32[]{:S(2)}, u32[]{:S(2)}) collective-permute-start(bf16[64,4096]{1,0:T(8,128)(2,1)} %get-tuple-element.16), channel_id=1, source_target_pairs={{0,1},{1,2},{2,3},{3,0},{4,5},{5,6},{6,7},{7,4},{8,9},{9,10},{10,1... | collective-permute-start | bytes 1572872 | tf_op jit(solution)/shard_map/ppermute | solution.py:37
  4.8 2.5 %collective-permute-start.1 = (bf16[64,4096]{1,0:T(8,128)(2,1)}, bf16[64,4096]{1,0:T(8,128)(2,1)S(1)}, u32[]{:S(2)}, u32[]{:S(2)}) collective-permute-start(bf16[64,4096]{1,0:T(8,128)(2,1)} %get-tuple-element.17), channel_id=1, source_target_pairs={{0,2},{1,3},{2,0},{3,1},{4,6},{5,7},{6,4},{7,5},{8,10},{9,11},{10,... | collective-permute-start | bytes 1572872 | tf_op jit(solution)/shard_map/ppermute | solution.py:37
  7.2 1.2 collective-permute-start.2
  8.5 0.1 fusion.22
  8.6 0.3 fusion.21
  9.0 0.2 fusion.4
  9.2 0.2 fusion.2
  9.5 1.5 broadcast_in_dim.33
  11.0 11.2 %all-to-all-start = ((bf16[32,4,4096]{2,1,0:T(4,128)(2,1)}), bf16[32,4,4096]{2,1,0:T(4,128)(2,1)S(1)}, u32[]{:S(2)}, u32[]{:S(2)}) async-start(bf16[32,4,4096]{2,1,0:T(4,128)(2,1)} %broadcast_in_dim.33), calls=%async_computation | async-start | bytes 2097152 | tf_op jit(solution)/shard_map/all_to_all | solution.py:42
  22.2 1.1 dynamic-slice_bitcast_fusion
  23.3 6.7 %collective-permute-done.1 = bf16[64,4096]{1,0:T(8,128)(2,1)S(1)} collective-permute-done((bf16[64,4096]{1,0:T(8,128)(2,1)}, bf16[64,4096]{1,0:T(8,128)(2,1)S(1)}, u32[]{:S(2)}, u32[]{:S(2)}) %collective-permute-start.1) | collective-permute-done | bytes 524320 | tf_op jit(solution)/shard_map/ppermute | solution.py:37
  30.0 1.5 pad_maximum_fusion
  31.5 1.5 collective-permute-start.3
  33.0 0.1 convolution_convert_fusion
  33.4 0.5 collective-permute-start.9
  34.0 0.4 collective-permute-start.8
  34.4 2.5 %collective-permute-done.7 = bf16[64,256]{1,0:T(8,128)(2,1)S(1)} collective-permute-done((bf16[64,256]{1,0:T(8,128)(2,1)S(1)}, bf16[64,256]{1,0:T(8,128)(2,1)S(1)}, u32[]{:S(2)}, u32[]{:S(2)}) %collective-permute-start.7) | collective-permute-done | bytes 32800 | tf_op jit(solution)/shard_map/ppermute | solution.py:33
  36.9 9.8 %all-to-all-done = bf16[32,4,4096]{2,1,0:T(4,128)(2,1)S(1)} async-done(((bf16[32,4,4096]{2,1,0:T(4,128)(2,1)}), bf16[32,4,4096]{2,1,0:T(4,128)(2,1)S(1)}, u32[]{:S(2)}, u32[]{:S(2)}) %all-to-all-start) | async-done | bytes 1048608 | tf_op jit(solution)/shard_map/all_to_all | solution.py:42
  46.7 0.3 reshape.63
  46.9 2.3 %fusion.23 = f32[4,64,128]{2,1,0:T(8,128)S(1)} fusion(bf16[4,64,4096]{2,1,0:T(8,128)(2,1)} %bitcast.3, bf16[128,4096,1]{1,0,2:T(8,128)(2,1)S(1)} %reshape.63), kind=kOutput, calls=%fused_computation.57 | convolution fusion | flops 268435456 | bytes 3276800 | tf_op jit(solution)/shard_map/dot_general | solution.py:300
  49.3 2.3 %fusion.24 = f32[4,64,128]{2,1,0:T(8,128)S(1)} fusion(bf16[4,64,4096]{2,1,0:T(8,128)(2,1)} %bitcast.6, bf16[128,4096,1]{1,0,2:T(8,128)(2,1)S(1)} %reshape.63), kind=kOutput, calls=%fused_computation.58 | convolution fusion | flops 268435456 | bytes 3276800 | tf_op jit(solution)/shard_map/dot_general | solution.py:300
  51.6 0.4 collective-permute-start.6
  52.0 1.1 collective-permute-start.5
  53.2 2.5 %collective-permute-done.6.c_ref = bf16[128,128]{1,0:T(8,128)(2,1)S(1)} collective-permute-done((bf16[128,128]{1,0:T(8,128)(2,1)S(1)}, bf16[128,128]{1,0:T(8,128)(2,1)S(1)}, u32[]{:S(2)}, u32[]{:S(2)}) %collective-permute-start.6) | collective-permute-done | bytes 32800 | tf_op jit(solution)/shard_map/ppermute | solution.py:37
  55.7 0.7 collective-permute-done.5.b_ref
  56.4 2.1 %collective-permute-done.4.a_ref = bf16[128,128]{1,0:T(8,128)(2,1)S(1)} collective-permute-done((bf16[128,128]{1,0:T(8,128)(2,1)S(1)}, bf16[128,128]{1,0:T(8,128)(2,1)S(1)}, u32[]{:S(2)}, u32[]{:S(2)}) %collective-permute-start.4) | collective-permute-done | bytes 32800 | tf_op jit(solution)/shard_map/ppermute | solution.py:37
  58.4 1.1 shard_map.128
  59.5 8.8 %all-to-all-start.1 = ((bf16[32,144,128]{2,1,0:T(8,128)(2,1)}), bf16[32,144,128]{2,1,0:T(8,128)(2,1)S(1)}, u32[]{:S(2)}, u32[]{:S(2)}) async-start(bf16[32,144,128]{2,1,0:T(8,128)(2,1)} %get-tuple-element.22), calls=%async_computation.1 | async-start | bytes 2359296 | tf_op jit(solution)/shard_map/all_to_all | solution.py:42
  68.5 23.9 %all-to-all-done.1.refs_4_ = bf16[32,144,128]{2,1,0:T(8,128)(2,1)S(1)} async-done(((bf16[32,144,128]{2,1,0:T(8,128)(2,1)}), bf16[32,144,128]{2,1,0:T(8,128)(2,1)S(1)}, u32[]{:S(2)}, u32[]{:S(2)}) %all-to-all-start.1) | async-done | bytes 1179680 | tf_op jit(solution)/shard_map/all_to_all | solution.py:42
  92.4 9.7 %shard_map.130 = (bf16[432,128]{1,0:T(8,128)(2,1)S(1)}, bf16[432,128]{1,0:T(8,128)(2,1)S(1)}, bf16[432,128]{1,0:T(8,128)(2,1)S(1)}, bf16[432,128]{1,0:T(8,128)(2,1)S(1)}) custom-call(s32[1]{0:T(128)} %bitcast.13.a_step, s32[1]{0:T(128)} %bitcast.14.b_step, s32[1]{0:T(128)} %bitcast.15.c_step, s32[1]{0:T(128)} %bitcast.16.d_step, bf16[416,4096]{1,0:T(8,128)(2,1)} %bitcast.53, ...), custom_call_target="tpu_custom_call" | custom-call | tf_op jit(solution)/shard_map/pallas_call | solution.py:330
  102.1 0.4 collective-permute-start.11
  102.5 3.8 %collective-permute-start.12 = (bf16[432,128]{1,0:T(8,128)(2,1)S(1)}, bf16[432,128]{1,0:T(8,128)(2,1)S(1)}, u32[]{:S(2)}, u32[]{:S(2)}) collective-permute-start(bf16[432,128]{1,0:T(8,128)(2,1)S(1)} %get-tuple-element.25), channel_id=1, source_target_pairs={{0,2},{1,3},{2,0},{3,1},{4,6},{5,7},{6,4},{7,5},{8,10},{9,11},{10,... | collective-permute-start | bytes 331784 | tf_op jit(solution)/shard_map/ppermute | solution.py:37
  106.3 1.0 collective-permute-done.11.b_ref
  107.3 2.4 %collective-permute-done.12.c_ref = bf16[432,128]{1,0:T(8,128)(2,1)S(1)} collective-permute-done((bf16[432,128]{1,0:T(8,128)(2,1)S(1)}, bf16[432,128]{1,0:T(8,128)(2,1)S(1)}, u32[]{:S(2)}, u32[]{:S(2)}) %collective-permute-start.12) | collective-permute-done | bytes 110624 | tf_op jit(solution)/shard_map/ppermute | solution.py:37
  109.7 0.3 collective-permute-done.13.d_ref
  110.0 1.7 %collective-permute-start.16 = (bf16[208,128]{1,0:T(8,128)(2,1)S(1)}, bf16[208,128]{1,0:T(8,128)(2,1)S(1)}, u32[]{:S(2)}, u32[]{:S(2)}) collective-permute-start(bf16[208,128]{1,0:T(8,128)(2,1)S(1)} %shard_map.131.a_ref), channel_id=1, source_target_pairs={{0,3},{1,0},{2,1},{3,2},{4,7},{5,4},{6,5},{7,6},{8,11},{9,8},{10,9... | collective-permute-start | bytes 159752 | tf_op jit(solution)/shard_map/ppermute | solution.py:37
  111.7 0.8 collective-permute-start.14
  112.5 3.0 %shard_map.129 = (bf16[416,4096]{1,0:T(8,128)(2,1)S(1)}, bf16[416,4096]{1,0:T(8,128)(2,1)S(1)}) custom-call(bf16[416,4096]{1,0:T(8,128)(2,1)} %refs_0_.1, bf16[416,4096]{1,0:T(8,128)(2,1)} %collective-permute-done.8.refs_1_), custom_call_target="tpu_custom_call" | custom-call | tf_op jit(solution)/shard_map/pallas_call | solution.py:157
  115.6 1.6 collective-permute-done.15.c_ref
  117.1 0.8 collective-permute-done.14.b_ref
  117.9 2.9 %shard_map.132 = bf16[32,128,128]{2,1,0:T(8,128)(2,1)} custom-call(s32[4]{0:T(128)S(1)} %fusion.15.places_ref, bf16[416,4096]{1,0:T(8,128)(2,1)S(1)} %get-tuple-element.20.own_ref, bf16[416,4096]{1,0:T(8,128)(2,1)S(1)} %get-tuple-element.21.other_ref, bf16[208,128]{1,0:T(8,128)(2,1)S(1)} %shard_map.131.a_ref, ...), custom_call_target="tpu_custom_call" | custom-call | tf_op jit(solution)/shard_map/pallas_call | solution.py:358
  120.8 7.1 %all-to-all-start.2 = ((bf16[32,128,128]{2,1,0:T(8,128)(2,1)}), bf16[32,128,128]{2,1,0:T(8,128)(2,1)S(1)}, u32[]{:S(2)}, u32[]{:S(2)}) async-start(bf16[32,128,128]{2,1,0:T(8,128)(2,1)} %shard_map.132), calls=%async_computation.2 | async-start | bytes 2097152 | tf_op jit(solution)/shard_map/all_to_all | solution.py:42
  127.9 18.0 %all-to-all-done.2 = bf16[32,128,128]{2,1,0:T(8,128)(2,1)S(1)} async-done(((bf16[32,128,128]{2,1,0:T(8,128)(2,1)}), bf16[32,128,128]{2,1,0:T(8,128)(2,1)S(1)}, u32[]{:S(2)}, u32[]{:S(2)}) %all-to-all-start.2) | async-done | bytes 1048608 | tf_op jit(solution)/shard_map/all_to_all | solution.py:42
  145.9 0.2 convert_reduce_fusion
  146.2 11.3 %collective-permute-start.17 = (bf16[64,128]{1,0:T(8,128)(2,1)S(1)}, bf16[64,128]{1,0:T(8,128)(2,1)S(1)}, u32[]{:S(2)}, u32[]{:S(2)}) collective-permute-start(bf16[64,128]{1,0:T(8,128)(2,1)S(1)} %get-tuple-element.33), channel_id=1, source_target_pairs={{0,4},{4,0},{8,12},{12,8},{16,20},{20,16},{24,28},{28,24},{32,36},... | collective-permute-start | bytes 49160 | tf_op jit(solution)/shard_map/ppermute | solution.py:33
  157.5 0.8 collective-permute-done.17
  158.4 0.8 fusion.3
  (50 shorter events, 0.8 us)
Async XLA Ops:
  0.0 8.6 %copy-start = (bf16[4,2,256,128]{3,2,1,0:T(8,128)(2,1)S(1)}, bf16[4,2,256,128]{3,2,1,0:T(8,128)(2,1)}, u32[]{:S(2)}) copy-start(bf16[4,2,256,128]{3,2,1,0:T(8,128)(2,1)} %param.14) | copy-start | bytes 1572868
  0.0 8.4 %copy-start.8 = (s32[4]{0:T(128)S(1)}, s32[4]{0:T(128)}, u32[]{:S(2)}) copy-start(s32[4]{0:T(128)} %param.18) | copy-start | bytes 52
  0.0 8.5 %copy-start.4 = (bf16[4,256]{1,0:T(4,128)(2,1)S(1)}, bf16[4,256]{1,0:T(4,128)(2,1)}, u32[]{:S(2)}) copy-start(bf16[4,256]{1,0:T(4,128)(2,1)} %param.16) | copy-start | bytes 6148
  0.0 8.5 %copy-start.5 = (bf16[4,256]{1,0:T(4,128)(2,1)S(1)}, bf16[4,256]{1,0:T(4,128)(2,1)}, u32[]{:S(2)}) copy-start(bf16[4,256]{1,0:T(4,128)(2,1)} %param.17) | copy-start | bytes 6148
  0.0 8.5 %copy-start.2 = (bf16[4,4096]{1,0:T(4,128)(2,1)S(1)}, bf16[4,4096]{1,0:T(4,128)(2,1)}, u32[]{:S(2)}) copy-start(bf16[4,4096]{1,0:T(4,128)(2,1)} %param.13) | copy-start | bytes 98308
  0.0 9.2 %copy-start.7 = (bf16[4,2,256,128]{3,2,1,0:T(8,128)(2,1)S(1)}, bf16[4,2,256,128]{3,2,1,0:T(8,128)(2,1)}, u32[]{:S(2)}) copy-start(bf16[4,2,256,128]{3,2,1,0:T(8,128)(2,1)} %param.15) | copy-start | bytes 1572868
  2.7 20.7 %collective-permute-start = (bf16[64,4096]{1,0:T(8,128)(2,1)}, bf16[64,4096]{1,0:T(8,128)(2,1)S(1)}, u32[]{:S(2)}, u32[]{:S(2)}) collective-permute-start(bf16[64,4096]{1,0:T(8,128)(2,1)} %get-tuple-element.16), channel_id=1, source_target_pairs={{0,1},{1,2},{2,3},{3,0},{4,5},{5,6},{6,7},{7,4},{8,9},{9,10},{10,1... | collective-permute-start | bytes 1572872 | tf_op jit(solution)/shard_map/ppermute | solution.py:37
  4.8 25.2 %collective-permute-start.1 = (bf16[64,4096]{1,0:T(8,128)(2,1)}, bf16[64,4096]{1,0:T(8,128)(2,1)S(1)}, u32[]{:S(2)}, u32[]{:S(2)}) collective-permute-start(bf16[64,4096]{1,0:T(8,128)(2,1)} %get-tuple-element.17), channel_id=1, source_target_pairs={{0,2},{1,3},{2,0},{3,1},{4,6},{5,7},{6,4},{7,5},{8,10},{9,11},{10,... | collective-permute-start | bytes 1572872 | tf_op jit(solution)/shard_map/ppermute | solution.py:37
  7.2 22.8 %collective-permute-start.2 = (bf16[64,4096]{1,0:T(8,128)(2,1)}, bf16[64,4096]{1,0:T(8,128)(2,1)S(1)}, u32[]{:S(2)}, u32[]{:S(2)}) collective-permute-start(bf16[64,4096]{1,0:T(8,128)(2,1)} %get-tuple-element.18), channel_id=1, source_target_pairs={{0,3},{1,0},{2,1},{3,2},{4,7},{5,4},{6,5},{7,6},{8,11},{9,8},{10,9... | collective-permute-start | bytes 1572872 | tf_op jit(solution)/shard_map/ppermute | solution.py:37
  11.0 35.7 %all-to-all-start = ((bf16[32,4,4096]{2,1,0:T(4,128)(2,1)}), bf16[32,4,4096]{2,1,0:T(4,128)(2,1)S(1)}, u32[]{:S(2)}, u32[]{:S(2)}) async-start(bf16[32,4,4096]{2,1,0:T(4,128)(2,1)} %broadcast_in_dim.33), calls=%async_computation | async-start | bytes 2097152 | tf_op jit(solution)/shard_map/all_to_all | solution.py:42
  23.3 9.8 %copy-start.1 = (bf16[256,256]{1,0:T(8,128)(2,1)S(1)}, bf16[256,256]{1,0:T(8,128)(2,1)}, u32[]{:S(2)}) copy-start(bf16[256,256]{1,0:T(8,128)(2,1)} %constant.92.clone) | copy-start | bytes 393220
  23.3 9.7 %copy-start.3 = (bf16[256,64]{0,1:T(8,128)(2,1)S(1)}, bf16[256,64]{0,1:T(8,128)(2,1)}, u32[]{:S(2)}) copy-start(bf16[256,64]{0,1:T(8,128)(2,1)} %param.19) | copy-start | bytes 98308
  23.3 9.9 %copy-start.6 = (bf16[64]{0:T(256)(128)(2,1)S(1)}, bf16[64]{0:T(256)(128)(2,1)}, u32[]{:S(2)}) copy-start(bf16[64]{0:T(256)(128)(2,1)} %param.21) | copy-start | bytes 388
  31.5 17.8 %collective-permute-start.3 = (bf16[256,4096]{1,0:T(8,128)(2,1)}, bf16[256,4096]{1,0:T(8,128)(2,1)}, u32[]{:S(2)}, u32[]{:S(2)}) collective-permute-start(bf16[256,4096]{1,0:T(8,128)(2,1)} %pad_maximum_fusion), channel_id=1, source_target_pairs={{0,4},{4,0},{8,12},{12,8},{16,20},{20,16},{24,28},{28,24},{32,36},... | collective-permute-start | bytes 6291464 | tf_op jit(solution)/shard_map/ppermute | solution.py:33
  33.3 3.6 %collective-permute-start.7 = (bf16[64,256]{1,0:T(8,128)(2,1)S(1)}, bf16[64,256]{1,0:T(8,128)(2,1)S(1)}, u32[]{:S(2)}, u32[]{:S(2)}) collective-permute-start(bf16[64,256]{1,0:T(8,128)(2,1)S(1)} %pad_maximum_fusion.1), channel_id=1, source_target_pairs={{0,4},{4,0},{8,12},{12,8},{16,20},{20,16},{24,28},{28,24},{32,36},... | collective-permute-start | bytes 98312 | tf_op jit(solution)/shard_map/ppermute | solution.py:33
  33.4 35.1 %collective-permute-start.9 = (bf16[416,4096]{1,0:T(8,128)(2,1)}, bf16[416,4096]{1,0:T(8,128)(2,1)}, u32[]{:S(2)}, u32[]{:S(2)}) collective-permute-start(bf16[416,4096]{1,0:T(8,128)(2,1)} %bitcast.52), channel_id=1, source_target_pairs={{0,4},{4,0},{8,12},{12,8},{16,20},{20,16},{24,28},{28,24},{32,36},... | collective-permute-start | bytes 10223624 | tf_op jit(solution)/shard_map/ppermute | solution.py:33
  33.9 34.6 %collective-permute-start.10 = (bf16[416,4096]{1,0:T(8,128)(2,1)}, bf16[416,4096]{1,0:T(8,128)(2,1)}, u32[]{:S(2)}, u32[]{:S(2)}) collective-permute-start(bf16[416,4096]{1,0:T(8,128)(2,1)} %bitcast.54), channel_id=1, source_target_pairs={{0,4},{4,0},{8,12},{12,8},{16,20},{20,16},{24,28},{28,24},{32,36},... | collective-permute-start | bytes 10223624 | tf_op jit(solution)/shard_map/ppermute | solution.py:33
  34.0 78.5 %collective-permute-start.8 = (bf16[416,4096]{1,0:T(8,128)(2,1)}, bf16[416,4096]{1,0:T(8,128)(2,1)}, u32[]{:S(2)}, u32[]{:S(2)}) collective-permute-start(bf16[416,4096]{1,0:T(8,128)(2,1)} %refs_0_.1), channel_id=1, source_target_pairs={{0,4},{4,0},{8,12},{12,8},{16,20},{20,16},{24,28},{28,24},{32,36},... | collective-permute-start | bytes 10223624 | tf_op jit(solution)/shard_map/ppermute | solution.py:33
  51.6 4.1 %collective-permute-start.6 = (bf16[128,128]{1,0:T(8,128)(2,1)S(1)}, bf16[128,128]{1,0:T(8,128)(2,1)S(1)}, u32[]{:S(2)}, u32[]{:S(2)}) collective-permute-start(bf16[128,128]{1,0:T(8,128)(2,1)S(1)} %get-tuple-element.29), channel_id=1, source_target_pairs={{0,1},{1,2},{2,3},{3,0},{4,5},{5,6},{6,7},{7,4},{8,9},{9,10},{10,1... | collective-permute-start | bytes 98312 | tf_op jit(solution)/shard_map/ppermute | solution.py:37
  52.0 4.4 %collective-permute-start.5 = (bf16[128,128]{1,0:T(8,128)(2,1)S(1)}, bf16[128,128]{1,0:T(8,128)(2,1)S(1)}, u32[]{:S(2)}, u32[]{:S(2)}) collective-permute-start(bf16[128,128]{1,0:T(8,128)(2,1)S(1)} %get-tuple-element.30), channel_id=1, source_target_pairs={{0,2},{1,3},{2,0},{3,1},{4,6},{5,7},{6,4},{7,5},{8,10},{9,11},{10,... | collective-permute-start | bytes 98312 | tf_op jit(solution)/shard_map/ppermute | solution.py:37
  55.7 2.8 %collective-permute-start.4 = (bf16[128,128]{1,0:T(8,128)(2,1)S(1)}, bf16[128,128]{1,0:T(8,128)(2,1)S(1)}, u32[]{:S(2)}, u32[]{:S(2)}) collective-permute-start(bf16[128,128]{1,0:T(8,128)(2,1)S(1)} %get-tuple-element.31), channel_id=1, source_target_pairs={{0,3},{1,0},{2,1},{3,2},{4,7},{5,4},{6,5},{7,6},{8,11},{9,8},{10,9... | collective-permute-start | bytes 98312 | tf_op jit(solution)/shard_map/ppermute | solution.py:37
  59.5 32.8 %all-to-all-start.1 = ((bf16[32,144,128]{2,1,0:T(8,128)(2,1)}), bf16[32,144,128]{2,1,0:T(8,128)(2,1)S(1)}, u32[]{:S(2)}, u32[]{:S(2)}) async-start(bf16[32,144,128]{2,1,0:T(8,128)(2,1)} %get-tuple-element.22), calls=%async_computation.1 | async-start | bytes 2359296 | tf_op jit(solution)/shard_map/all_to_all | solution.py:42
  102.1 5.2 %collective-permute-start.11 = (bf16[432,128]{1,0:T(8,128)(2,1)S(1)}, bf16[432,128]{1,0:T(8,128)(2,1)S(1)}, u32[]{:S(2)}, u32[]{:S(2)}) collective-permute-start(bf16[432,128]{1,0:T(8,128)(2,1)S(1)} %get-tuple-element.24), channel_id=1, source_target_pairs={{0,1},{1,2},{2,3},{3,0},{4,5},{5,6},{6,7},{7,4},{8,9},{9,10},{10,1... | collective-permute-start | bytes 331784 | tf_op jit(solution)/shard_map/ppermute | solution.py:37
  102.5 7.2 %collective-permute-start.12 = (bf16[432,128]{1,0:T(8,128)(2,1)S(1)}, bf16[432,128]{1,0:T(8,128)(2,1)S(1)}, u32[]{:S(2)}, u32[]{:S(2)}) collective-permute-start(bf16[432,128]{1,0:T(8,128)(2,1)S(1)} %get-tuple-element.25), channel_id=1, source_target_pairs={{0,2},{1,3},{2,0},{3,1},{4,6},{5,7},{6,4},{7,5},{8,10},{9,11},{10,... | collective-permute-start | bytes 331784 | tf_op jit(solution)/shard_map/ppermute | solution.py:37
  106.3 3.6 %collective-permute-start.13 = (bf16[432,128]{1,0:T(8,128)(2,1)S(1)}, bf16[432,128]{1,0:T(8,128)(2,1)S(1)}, u32[]{:S(2)}, u32[]{:S(2)}) collective-permute-start(bf16[432,128]{1,0:T(8,128)(2,1)S(1)} %get-tuple-element.26), channel_id=1, source_target_pairs={{0,3},{1,0},{2,1},{3,2},{4,7},{5,4},{6,5},{7,6},{8,11},{9,8},{10,9... | collective-permute-start | bytes 331784 | tf_op jit(solution)/shard_map/ppermute | solution.py:37
  110.0 5.5 %collective-permute-start.16 = (bf16[208,128]{1,0:T(8,128)(2,1)S(1)}, bf16[208,128]{1,0:T(8,128)(2,1)S(1)}, u32[]{:S(2)}, u32[]{:S(2)}) collective-permute-start(bf16[208,128]{1,0:T(8,128)(2,1)S(1)} %shard_map.131.a_ref), channel_id=1, source_target_pairs={{0,3},{1,0},{2,1},{3,2},{4,7},{5,4},{6,5},{7,6},{8,11},{9,8},{10,9... | collective-permute-start | bytes 159752 | tf_op jit(solution)/shard_map/ppermute | solution.py:37
  111.7 5.4 %collective-permute-start.15 = (bf16[208,128]{1,0:T(8,128)(2,1)S(1)}, bf16[208,128]{1,0:T(8,128)(2,1)S(1)}, u32[]{:S(2)}, u32[]{:S(2)}) collective-permute-start(bf16[208,128]{1,0:T(8,128)(2,1)S(1)} %shard_map.131.a_ref), channel_id=1, source_target_pairs={{0,2},{1,3},{2,0},{3,1},{4,6},{5,7},{6,4},{7,5},{8,10},{9,11},{10,... | collective-permute-start | bytes 159752 | tf_op jit(solution)/shard_map/ppermute | solution.py:37
  111.7 6.2 %collective-permute-start.14 = (bf16[208,128]{1,0:T(8,128)(2,1)S(1)}, bf16[208,128]{1,0:T(8,128)(2,1)S(1)}, u32[]{:S(2)}, u32[]{:S(2)}) collective-permute-start(bf16[208,128]{1,0:T(8,128)(2,1)S(1)} %shard_map.131.a_ref), channel_id=1, source_target_pairs={{0,1},{1,2},{2,3},{3,0},{4,5},{5,6},{6,7},{7,4},{8,9},{9,10},{10,1... | collective-permute-start | bytes 159752 | tf_op jit(solution)/shard_map/ppermute | solution.py:37
  120.8 25.1 %all-to-all-start.2 = ((bf16[32,128,128]{2,1,0:T(8,128)(2,1)}), bf16[32,128,128]{2,1,0:T(8,128)(2,1)S(1)}, u32[]{:S(2)}, u32[]{:S(2)}) async-start(bf16[32,128,128]{2,1,0:T(8,128)(2,1)} %shard_map.132), calls=%async_computation.2 | async-start | bytes 2097152 | tf_op jit(solution)/shard_map/all_to_all | solution.py:42
  146.2 12.2 %collective-permute-start.17 = (bf16[64,128]{1,0:T(8,128)(2,1)S(1)}, bf16[64,128]{1,0:T(8,128)(2,1)S(1)}, u32[]{:S(2)}, u32[]{:S(2)}) collective-permute-start(bf16[64,128]{1,0:T(8,128)(2,1)S(1)} %get-tuple-element.33), channel_id=1, source_target_pairs={{0,4},{4,0},{8,12},{12,8},{16,20},{20,16},{24,28},{28,24},{32,36},... | collective-permute-start | bytes 49160 | tf_op jit(solution)/shard_map/ppermute | solution.py:33

commit v3 on v2

--- a/solution.py
+++ b/solution.py
@@ -128,7 +128,7 @@
 
 
 def cut(place, weights, width):
-    piece = jax.ShapeDtypeStruct((weights.shape[0], width), weights.dtype)
+    piece = pltpu.VMEM((weights.shape[0], width), weights.dtype)
     return pl.pallas_call(
         cut_kernel,
         out_shape=[piece] * (QUARTERS - 1),
@@ -204,12 +204,16 @@
         features[p * PAIR : (p + 1) * PAIR, :] = blocks_ref[p, :PAIR, :]
         squares = squares + blocks_ref[p, PAIR:, :].astype(F32)
     tail = spread(squares[0:1] + squares[1:2])
+    rows = 2 * units // PARTS
     for place, group in enumerate(copies):
-        for copy in group:
+        for part, copy in enumerate(group):
             copy.wait()
-        sums[place * 2 * units : (place + 1) * 2 * units, :] = jnp.dot(
-            buffer[place], features[...], preferred_element_type=F32
-        )
+            start = place * 2 * units + part * rows
+            sums[start : start + rows, :] = jnp.dot(
+                buffer[place, part * rows : (part + 1) * rows, :],
+                features[...],
+                preferred_element_type=F32,
+            )
     for part in range(QUARTERS):
         start = (part // 2 * 4 + part % 2) * units
         gates, ups = slice(start, start + units), slice(start + 2 * units, start + 3 * units)

time: 160 us -> 155 us (0.969)
  Pallas kernels: 19.4 us -> 15 us
    pallas_call x1, Pallas kernels: 9.73 us -> 6.4 us  [per_device(): kernel_call(expand_kernel, [message] * QUARTERS, scratch=[pltpu.VMEM((wid...]
  transfers between devices with their start and end apart: 21 -> 21, of which waited for: 14 -> 14; matrix products, arithmetic and copies ran while one was open for 6% -> 8% of each run, Pallas kernels for 9% -> 7%
where the time goes in v3:
time: 155 us
  waiting for transfers between devices  71.5 us (46%)
  starting transfers between devices  55 us (35%)
  Pallas kernels  15 us (10%)
  matrix products  6.23 us (4%)
  other arithmetic  3.44 us (2%)
  local copies, waits for them, and re-layouts  3.13 us (2%)
    all_to_all x3, waiting for transfers between devices, plane_exchange(): lax.all_to_all(blocks, 'gx', 0, 0, axis_index_groups=groups, tiled=True)  50.3 us
    all_to_all x3, starting transfers between devices, plane_exchange(): lax.all_to_all(blocks, 'gx', 0, 0, axis_index_groups=groups, tiled=True)  27.2 us
    ppermute x12, waiting for transfers between devices, along_gy(): lax.ppermute(value, 'gy', [(i, (i + step) % QUARTERS) for i in range(QUAR...  17.8 us
    ppermute x6, starting transfers between devices, to_core(): return lax.ppermute(value, 'gx', [(g, g ^ 1) for g in range(PLANE * CORES)])  14 us
    ppermute x12, starting transfers between devices, along_gy(): lax.ppermute(value, 'gy', [(i, (i + step) % QUARTERS) for i in range(QUAR...  13.9 us
    pallas_call x1, Pallas kernels, per_device(): kernel_call(expand_kernel, [message] * QUARTERS, scratch=[pltpu.VMEM((wid...  6.4 us
    dot_general x2, matrix products, project(): lax.dot_general(weights, rows, (((1,), (1,)), ((), ())), preferred_elemen...  4.59 us
    ppermute x6, waiting for transfers between devices, to_core(): return lax.ppermute(value, 'gx', [(g, g ^ 1) for g in range(PLANE * CORES)])  3.36 us
  transfers between devices with their start and end apart: 21, of which 14 were waited for; matrix products, arithmetic and copies ran while one was open for 8% of the time, Pallas kernels for 7%

profile of v3, /device:TPU:1, one launch (start us, length us, event | category | flops | bytes accessed | tf_op | source)
XLA Modules:
  0.0 154.7 jit_solution(14254802151697232840)
XLA Ops:
  0.0 1.5 shard_map.127
  1.5 2.1 %collective-permute-start = (bf16[64,4096]{1,0:T(8,128)(2,1)S(1)}, bf16[64,4096]{1,0:T(8,128)(2,1)}, u32[]{:S(2)}, u32[]{:S(2)}) collective-permute-start(bf16[64,4096]{1,0:T(8,128)(2,1)S(1)} %get-tuple-element.16), channel_id=1, source_target_pairs={{0,1},{1,2},{2,3},{3,0},{4,5},{5,6},{6,7},{7,4},{8,9},{9,10},{10,1... | collective-permute-start | bytes 1572872 | tf_op jit(solution)/shard_map/ppermute | solution.py:37
  3.6 2.5 %collective-permute-start.1 = (bf16[64,4096]{1,0:T(8,128)(2,1)S(1)}, bf16[64,4096]{1,0:T(8,128)(2,1)}, u32[]{:S(2)}, u32[]{:S(2)}) collective-permute-start(bf16[64,4096]{1,0:T(8,128)(2,1)S(1)} %get-tuple-element.17), channel_id=1, source_target_pairs={{0,2},{1,3},{2,0},{3,1},{4,6},{5,7},{6,4},{7,5},{8,10},{9,11},{10,... | collective-permute-start | bytes 1572872 | tf_op jit(solution)/shard_map/ppermute | solution.py:37
  6.1 1.2 collective-permute-start.2
  7.4 0.1 fusion.22
  7.5 0.3 fusion.21
  7.9 0.2 fusion.4
  8.1 0.2 fusion.2
  8.4 1.5 broadcast_in_dim.33
  9.8 11.2 %all-to-all-start = ((bf16[32,4,4096]{2,1,0:T(4,128)(2,1)}), bf16[32,4,4096]{2,1,0:T(4,128)(2,1)S(1)}, u32[]{:S(2)}, u32[]{:S(2)}) async-start(bf16[32,4,4096]{2,1,0:T(4,128)(2,1)} %broadcast_in_dim.33), calls=%async_computation | async-start | bytes 2097152 | tf_op jit(solution)/shard_map/all_to_all | solution.py:42
  21.1 1.1 dynamic-slice_bitcast_fusion
  22.2 6.6 %collective-permute-done.1 = bf16[64,4096]{1,0:T(8,128)(2,1)} collective-permute-done((bf16[64,4096]{1,0:T(8,128)(2,1)S(1)}, bf16[64,4096]{1,0:T(8,128)(2,1)}, u32[]{:S(2)}, u32[]{:S(2)}) %collective-permute-start.1) | collective-permute-done | bytes 524320 | tf_op jit(solution)/shard_map/ppermute | solution.py:37
  28.8 2.9 %pad_maximum_fusion = bf16[256,4096]{1,0:T(8,128)(2,1)} fusion(bf16[64,4096]{1,0:T(8,128)(2,1)} %collective-permute-done.2, bf16[64,4096]{1,0:T(8,128)(2,1)} %collective-permute-done.1, bf16[64,4096]{1,0:T(8,128)(2,1)} %collective-permute-done, bf16[64,4096]{1,0:T(8,128)(2,1)S(1)} %dynamic-slice_bitcast_fusion), kind=kLoop, calls=%fused_computation | loop fusion | flops 8388608 | bytes 4194304 | tf_op jit(solution)/shard_map/concatenate | solution.py:284
  31.7 1.5 collective-permute-start.3
  33.2 0.1 convolution_convert_fusion
  33.6 0.5 collective-permute-start.9
  34.2 0.4 collective-permute-start.8
  34.6 2.5 %collective-permute-done.7 = bf16[64,256]{1,0:T(8,128)(2,1)S(1)} collective-permute-done((bf16[64,256]{1,0:T(8,128)(2,1)S(1)}, bf16[64,256]{1,0:T(8,128)(2,1)S(1)}, u32[]{:S(2)}, u32[]{:S(2)}) %collective-permute-start.7) | collective-permute-done | bytes 32800 | tf_op jit(solution)/shard_map/ppermute | solution.py:33
  37.1 8.4 %all-to-all-done = bf16[32,4,4096]{2,1,0:T(4,128)(2,1)S(1)} async-done(((bf16[32,4,4096]{2,1,0:T(4,128)(2,1)}), bf16[32,4,4096]{2,1,0:T(4,128)(2,1)S(1)}, u32[]{:S(2)}, u32[]{:S(2)}) %all-to-all-start) | async-done | bytes 1048608 | tf_op jit(solution)/shard_map/all_to_all | solution.py:42
  45.5 0.3 reshape.63
  45.8 2.3 %fusion.23 = f32[4,64,128]{2,1,0:T(8,128)S(1)} fusion(bf16[4,64,4096]{2,1,0:T(8,128)(2,1)} %bitcast.3, bf16[128,4096,1]{1,0,2:T(8,128)(2,1)S(1)} %reshape.63), kind=kOutput, calls=%fused_computation.57 | convolution fusion | flops 268435456 | bytes 3276800 | tf_op jit(solution)/shard_map/dot_general | solution.py:304
  48.1 2.3 %fusion.24 = f32[4,64,128]{2,1,0:T(8,128)S(1)} fusion(bf16[4,64,4096]{2,1,0:T(8,128)(2,1)} %bitcast.6, bf16[128,4096,1]{1,0,2:T(8,128)(2,1)S(1)} %reshape.63), kind=kOutput, calls=%fused_computation.58 | convolution fusion | flops 268435456 | bytes 3276800 | tf_op jit(solution)/shard_map/dot_general | solution.py:304
  50.5 0.4 collective-permute-start.6
  50.9 1.1 collective-permute-start.5
  52.0 2.5 %collective-permute-done.6.c_ref = bf16[128,128]{1,0:T(8,128)(2,1)S(1)} collective-permute-done((bf16[128,128]{1,0:T(8,128)(2,1)S(1)}, bf16[128,128]{1,0:T(8,128)(2,1)S(1)}, u32[]{:S(2)}, u32[]{:S(2)}) %collective-permute-start.6) | collective-permute-done | bytes 32800 | tf_op jit(solution)/shard_map/ppermute | solution.py:37
  54.5 0.7 collective-permute-done.5.b_ref
  55.2 2.1 %collective-permute-done.4.a_ref = bf16[128,128]{1,0:T(8,128)(2,1)S(1)} collective-permute-done((bf16[128,128]{1,0:T(8,128)(2,1)S(1)}, bf16[128,128]{1,0:T(8,128)(2,1)S(1)}, u32[]{:S(2)}, u32[]{:S(2)}) %collective-permute-start.4) | collective-permute-done | bytes 32800 | tf_op jit(solution)/shard_map/ppermute | solution.py:37
  57.3 1.1 shard_map.128
  58.4 8.8 %all-to-all-start.1 = ((bf16[32,144,128]{2,1,0:T(8,128)(2,1)}), bf16[32,144,128]{2,1,0:T(8,128)(2,1)S(1)}, u32[]{:S(2)}, u32[]{:S(2)}) async-start(bf16[32,144,128]{2,1,0:T(8,128)(2,1)} %get-tuple-element.22), calls=%async_computation.1 | async-start | bytes 2359296 | tf_op jit(solution)/shard_map/all_to_all | solution.py:42
  67.3 23.9 %all-to-all-done.1.refs_4_ = bf16[32,144,128]{2,1,0:T(8,128)(2,1)S(1)} async-done(((bf16[32,144,128]{2,1,0:T(8,128)(2,1)}), bf16[32,144,128]{2,1,0:T(8,128)(2,1)S(1)}, u32[]{:S(2)}, u32[]{:S(2)}) %all-to-all-start.1) | async-done | bytes 1179680 | tf_op jit(solution)/shard_map/all_to_all | solution.py:42
  91.2 6.4 %shard_map.130 = (bf16[432,128]{1,0:T(8,128)(2,1)S(1)}, bf16[432,128]{1,0:T(8,128)(2,1)S(1)}, bf16[432,128]{1,0:T(8,128)(2,1)S(1)}, bf16[432,128]{1,0:T(8,128)(2,1)S(1)}) custom-call(s32[1]{0:T(128)} %bitcast.13.a_step, s32[1]{0:T(128)} %bitcast.14.b_step, s32[1]{0:T(128)} %bitcast.15.c_step, s32[1]{0:T(128)} %bitcast.16.d_step, bf16[416,4096]{1,0:T(8,128)(2,1)} %bitcast.53, ...), custom_call_target="tpu_custom_call" | custom-call | tf_op jit(solution)/shard_map/pallas_call | solution.py:334
  97.7 0.3 collective-permute-start.11
  98.0 3.9 %collective-permute-start.12 = (bf16[432,128]{1,0:T(8,128)(2,1)S(1)}, bf16[432,128]{1,0:T(8,128)(2,1)S(1)}, u32[]{:S(2)}, u32[]{:S(2)}) collective-permute-start(bf16[432,128]{1,0:T(8,128)(2,1)S(1)} %get-tuple-element.25), channel_id=1, source_target_pairs={{0,2},{1,3},{2,0},{3,1},{4,6},{5,7},{6,4},{7,5},{8,10},{9,11},{10,... | collective-permute-start | bytes 331784 | tf_op jit(solution)/shard_map/ppermute | solution.py:37
  101.9 1.0 collective-permute-done.11.b_ref
  102.8 2.4 %collective-permute-done.12.c_ref = bf16[432,128]{1,0:T(8,128)(2,1)S(1)} collective-permute-done((bf16[432,128]{1,0:T(8,128)(2,1)S(1)}, bf16[432,128]{1,0:T(8,128)(2,1)S(1)}, u32[]{:S(2)}, u32[]{:S(2)}) %collective-permute-start.12) | collective-permute-done | bytes 110624 | tf_op jit(solution)/shard_map/ppermute | solution.py:37
  105.2 0.3 collective-permute-done.13.d_ref
  105.5 1.7 %collective-permute-start.16 = (bf16[208,128]{1,0:T(8,128)(2,1)S(1)}, bf16[208,128]{1,0:T(8,128)(2,1)S(1)}, u32[]{:S(2)}, u32[]{:S(2)}) collective-permute-start(bf16[208,128]{1,0:T(8,128)(2,1)S(1)} %shard_map.131.a_ref), channel_id=1, source_target_pairs={{0,3},{1,0},{2,1},{3,2},{4,7},{5,4},{6,5},{7,6},{8,11},{9,8},{10,9... | collective-permute-start | bytes 159752 | tf_op jit(solution)/shard_map/ppermute | solution.py:37
  107.2 0.8 collective-permute-start.14
  108.0 3.0 %shard_map.129 = (bf16[416,4096]{1,0:T(8,128)(2,1)S(1)}, bf16[416,4096]{1,0:T(8,128)(2,1)S(1)}) custom-call(bf16[416,4096]{1,0:T(8,128)(2,1)} %refs_0_.1, bf16[416,4096]{1,0:T(8,128)(2,1)} %collective-permute-done.8.refs_1_), custom_call_target="tpu_custom_call" | custom-call | tf_op jit(solution)/shard_map/pallas_call | solution.py:157
  111.1 1.6 %collective-permute-done.15.c_ref = bf16[208,128]{1,0:T(8,128)(2,1)S(1)} collective-permute-done((bf16[208,128]{1,0:T(8,128)(2,1)S(1)}, bf16[208,128]{1,0:T(8,128)(2,1)S(1)}, u32[]{:S(2)}, u32[]{:S(2)}) %collective-permute-start.15) | collective-permute-done | bytes 53280 | tf_op jit(solution)/shard_map/ppermute | solution.py:37
  112.6 0.8 collective-permute-done.14.b_ref
  113.5 2.9 %shard_map.132 = bf16[32,128,128]{2,1,0:T(8,128)(2,1)} custom-call(s32[4]{0:T(128)S(1)} %fusion.15.places_ref, bf16[416,4096]{1,0:T(8,128)(2,1)S(1)} %get-tuple-element.20.own_ref, bf16[416,4096]{1,0:T(8,128)(2,1)S(1)} %get-tuple-element.21.other_ref, bf16[208,128]{1,0:T(8,128)(2,1)S(1)} %shard_map.131.a_ref, ...), custom_call_target="tpu_custom_call" | custom-call | tf_op jit(solution)/shard_map/pallas_call | solution.py:362
  116.3 7.1 %all-to-all-start.2 = ((bf16[32,128,128]{2,1,0:T(8,128)(2,1)}), bf16[32,128,128]{2,1,0:T(8,128)(2,1)S(1)}, u32[]{:S(2)}, u32[]{:S(2)}) async-start(bf16[32,128,128]{2,1,0:T(8,128)(2,1)} %shard_map.132), calls=%async_computation.2 | async-start | bytes 2097152 | tf_op jit(solution)/shard_map/all_to_all | solution.py:42
  123.4 18.0 %all-to-all-done.2 = bf16[32,128,128]{2,1,0:T(8,128)(2,1)S(1)} async-done(((bf16[32,128,128]{2,1,0:T(8,128)(2,1)}), bf16[32,128,128]{2,1,0:T(8,128)(2,1)S(1)}, u32[]{:S(2)}, u32[]{:S(2)}) %all-to-all-start.2) | async-done | bytes 1048608 | tf_op jit(solution)/shard_map/all_to_all | solution.py:42
  141.4 0.2 convert_reduce_fusion
  141.7 11.3 %collective-permute-start.17 = (bf16[64,128]{1,0:T(8,128)(2,1)S(1)}, bf16[64,128]{1,0:T(8,128)(2,1)S(1)}, u32[]{:S(2)}, u32[]{:S(2)}) collective-permute-start(bf16[64,128]{1,0:T(8,128)(2,1)S(1)} %get-tuple-element.33), channel_id=1, source_target_pairs={{0,4},{4,0},{8,12},{12,8},{16,20},{20,16},{24,28},{28,24},{32,36},... | collective-permute-start | bytes 49160 | tf_op jit(solution)/shard_map/ppermute | solution.py:33
  153.1 0.8 collective-permute-done.17
  153.9 0.8 fusion.3
  (50 shorter events, 0.8 us)
Async XLA Ops:
  0.0 7.5 %copy-start = (bf16[4,2,256,128]{3,2,1,0:T(8,128)(2,1)S(1)}, bf16[4,2,256,128]{3,2,1,0:T(8,128)(2,1)}, u32[]{:S(2)}) copy-start(bf16[4,2,256,128]{3,2,1,0:T(8,128)(2,1)} %param.14) | copy-start | bytes 1572868
  0.0 7.2 %copy-start.8 = (s32[4]{0:T(128)S(1)}, s32[4]{0:T(128)}, u32[]{:S(2)}) copy-start(s32[4]{0:T(128)} %param.18) | copy-start | bytes 52
  0.0 7.3 %copy-start.4 = (bf16[4,256]{1,0:T(4,128)(2,1)S(1)}, bf16[4,256]{1,0:T(4,128)(2,1)}, u32[]{:S(2)}) copy-start(bf16[4,256]{1,0:T(4,128)(2,1)} %param.16) | copy-start | bytes 6148
  0.0 7.3 %copy-start.5 = (bf16[4,256]{1,0:T(4,128)(2,1)S(1)}, bf16[4,256]{1,0:T(4,128)(2,1)}, u32[]{:S(2)}) copy-start(bf16[4,256]{1,0:T(4,128)(2,1)} %param.17) | copy-start | bytes 6148
  0.0 7.3 %copy-start.2 = (bf16[4,4096]{1,0:T(4,128)(2,1)S(1)}, bf16[4,4096]{1,0:T(4,128)(2,1)}, u32[]{:S(2)}) copy-start(bf16[4,4096]{1,0:T(4,128)(2,1)} %param.13) | copy-start | bytes 98308
  0.0 8.0 %copy-start.7 = (bf16[4,2,256,128]{3,2,1,0:T(8,128)(2,1)S(1)}, bf16[4,2,256,128]{3,2,1,0:T(8,128)(2,1)}, u32[]{:S(2)}) copy-start(bf16[4,2,256,128]{3,2,1,0:T(8,128)(2,1)} %param.15) | copy-start | bytes 1572868
  1.5 20.7 %collective-permute-start = (bf16[64,4096]{1,0:T(8,128)(2,1)S(1)}, bf16[64,4096]{1,0:T(8,128)(2,1)}, u32[]{:S(2)}, u32[]{:S(2)}) collective-permute-start(bf16[64,4096]{1,0:T(8,128)(2,1)S(1)} %get-tuple-element.16), channel_id=1, source_target_pairs={{0,1},{1,2},{2,3},{3,0},{4,5},{5,6},{6,7},{7,4},{8,9},{9,10},{10,1... | collective-permute-start | bytes 1572872 | tf_op jit(solution)/shard_map/ppermute | solution.py:37
  3.6 25.1 %collective-permute-start.1 = (bf16[64,4096]{1,0:T(8,128)(2,1)S(1)}, bf16[64,4096]{1,0:T(8,128)(2,1)}, u32[]{:S(2)}, u32[]{:S(2)}) collective-permute-start(bf16[64,4096]{1,0:T(8,128)(2,1)S(1)} %get-tuple-element.17), channel_id=1, source_target_pairs={{0,2},{1,3},{2,0},{3,1},{4,6},{5,7},{6,4},{7,5},{8,10},{9,11},{10,... | collective-permute-start | bytes 1572872 | tf_op jit(solution)/shard_map/ppermute | solution.py:37
  6.1 22.7 %collective-permute-start.2 = (bf16[64,4096]{1,0:T(8,128)(2,1)S(1)}, bf16[64,4096]{1,0:T(8,128)(2,1)}, u32[]{:S(2)}, u32[]{:S(2)}) collective-permute-start(bf16[64,4096]{1,0:T(8,128)(2,1)S(1)} %get-tuple-element.18), channel_id=1, source_target_pairs={{0,3},{1,0},{2,1},{3,2},{4,7},{5,4},{6,5},{7,6},{8,11},{9,8},{10,9... | collective-permute-start | bytes 1572872 | tf_op jit(solution)/shard_map/ppermute | solution.py:37
  9.8 35.7 %all-to-all-start = ((bf16[32,4,4096]{2,1,0:T(4,128)(2,1)}), bf16[32,4,4096]{2,1,0:T(4,128)(2,1)S(1)}, u32[]{:S(2)}, u32[]{:S(2)}) async-start(bf16[32,4,4096]{2,1,0:T(4,128)(2,1)} %broadcast_in_dim.33), calls=%async_computation | async-start | bytes 2097152 | tf_op jit(solution)/shard_map/all_to_all | solution.py:42
  22.1 11.1 %copy-start.1 = (bf16[256,256]{1,0:T(8,128)(2,1)S(1)}, bf16[256,256]{1,0:T(8,128)(2,1)}, u32[]{:S(2)}) copy-start(bf16[256,256]{1,0:T(8,128)(2,1)} %constant.92.clone) | copy-start | bytes 393220
  22.1 11.1 %copy-start.3 = (bf16[256,64]{0,1:T(8,128)(2,1)S(1)}, bf16[256,64]{0,1:T(8,128)(2,1)}, u32[]{:S(2)}) copy-start(bf16[256,64]{0,1:T(8,128)(2,1)} %param.19) | copy-start | bytes 98308
  22.2 11.2 %copy-start.6 = (bf16[64]{0:T(256)(128)(2,1)S(1)}, bf16[64]{0:T(256)(128)(2,1)}, u32[]{:S(2)}) copy-start(bf16[64]{0:T(256)(128)(2,1)} %param.21) | copy-start | bytes 388
  31.7 16.4 %collective-permute-start.3 = (bf16[256,4096]{1,0:T(8,128)(2,1)}, bf16[256,4096]{1,0:T(8,128)(2,1)}, u32[]{:S(2)}, u32[]{:S(2)}) collective-permute-start(bf16[256,4096]{1,0:T(8,128)(2,1)} %pad_maximum_fusion), channel_id=1, source_target_pairs={{0,4},{4,0},{8,12},{12,8},{16,20},{20,16},{24,28},{28,24},{32,36},... | collective-permute-start | bytes 6291464 | tf_op jit(solution)/shard_map/ppermute | solution.py:33
  33.5 3.6 %collective-permute-start.7 = (bf16[64,256]{1,0:T(8,128)(2,1)S(1)}, bf16[64,256]{1,0:T(8,128)(2,1)S(1)}, u32[]{:S(2)}, u32[]{:S(2)}) collective-permute-start(bf16[64,256]{1,0:T(8,128)(2,1)S(1)} %pad_maximum_fusion.1), channel_id=1, source_target_pairs={{0,4},{4,0},{8,12},{12,8},{16,20},{20,16},{24,28},{28,24},{32,36},... | collective-permute-start | bytes 98312 | tf_op jit(solution)/shard_map/ppermute | solution.py:33
  33.6 33.7 %collective-permute-start.9 = (bf16[416,4096]{1,0:T(8,128)(2,1)}, bf16[416,4096]{1,0:T(8,128)(2,1)}, u32[]{:S(2)}, u32[]{:S(2)}) collective-permute-start(bf16[416,4096]{1,0:T(8,128)(2,1)} %bitcast.52), channel_id=1, source_target_pairs={{0,4},{4,0},{8,12},{12,8},{16,20},{20,16},{24,28},{28,24},{32,36},... | collective-permute-start | bytes 10223624 | tf_op jit(solution)/shard_map/ppermute | solution.py:33
  34.1 33.3 %collective-permute-start.10 = (bf16[416,4096]{1,0:T(8,128)(2,1)}, bf16[416,4096]{1,0:T(8,128)(2,1)}, u32[]{:S(2)}, u32[]{:S(2)}) collective-permute-start(bf16[416,4096]{1,0:T(8,128)(2,1)} %bitcast.54), channel_id=1, source_target_pairs={{0,4},{4,0},{8,12},{12,8},{16,20},{20,16},{24,28},{28,24},{32,36},... | collective-permute-start | bytes 10223624 | tf_op jit(solution)/shard_map/ppermute | solution.py:33
  34.2 73.8 %collective-permute-start.8 = (bf16[416,4096]{1,0:T(8,128)(2,1)}, bf16[416,4096]{1,0:T(8,128)(2,1)}, u32[]{:S(2)}, u32[]{:S(2)}) collective-permute-start(bf16[416,4096]{1,0:T(8,128)(2,1)} %refs_0_.1), channel_id=1, source_target_pairs={{0,4},{4,0},{8,12},{12,8},{16,20},{20,16},{24,28},{28,24},{32,36},... | collective-permute-start | bytes 10223624 | tf_op jit(solution)/shard_map/ppermute | solution.py:33
  50.5 4.1 %collective-permute-start.6 = (bf16[128,128]{1,0:T(8,128)(2,1)S(1)}, bf16[128,128]{1,0:T(8,128)(2,1)S(1)}, u32[]{:S(2)}, u32[]{:S(2)}) collective-permute-start(bf16[128,128]{1,0:T(8,128)(2,1)S(1)} %get-tuple-element.29), channel_id=1, source_target_pairs={{0,1},{1,2},{2,3},{3,0},{4,5},{5,6},{6,7},{7,4},{8,9},{9,10},{10,1... | collective-permute-start | bytes 98312 | tf_op jit(solution)/shard_map/ppermute | solution.py:37
  50.9 4.4 %collective-permute-start.5 = (bf16[128,128]{1,0:T(8,128)(2,1)S(1)}, bf16[128,128]{1,0:T(8,128)(2,1)S(1)}, u32[]{:S(2)}, u32[]{:S(2)}) collective-permute-start(bf16[128,128]{1,0:T(8,128)(2,1)S(1)} %get-tuple-element.30), channel_id=1, source_target_pairs={{0,2},{1,3},{2,0},{3,1},{4,6},{5,7},{6,4},{7,5},{8,10},{9,11},{10,... | collective-permute-start | bytes 98312 | tf_op jit(solution)/shard_map/ppermute | solution.py:37
  54.5 2.8 %collective-permute-start.4 = (bf16[128,128]{1,0:T(8,128)(2,1)S(1)}, bf16[128,128]{1,0:T(8,128)(2,1)S(1)}, u32[]{:S(2)}, u32[]{:S(2)}) collective-permute-start(bf16[128,128]{1,0:T(8,128)(2,1)S(1)} %get-tuple-element.31), channel_id=1, source_target_pairs={{0,3},{1,0},{2,1},{3,2},{4,7},{5,4},{6,5},{7,6},{8,11},{9,8},{10,9... | collective-permute-start | bytes 98312 | tf_op jit(solution)/shard_map/ppermute | solution.py:37
  58.4 32.8 %all-to-all-start.1 = ((bf16[32,144,128]{2,1,0:T(8,128)(2,1)}), bf16[32,144,128]{2,1,0:T(8,128)(2,1)S(1)}, u32[]{:S(2)}, u32[]{:S(2)}) async-start(bf16[32,144,128]{2,1,0:T(8,128)(2,1)} %get-tuple-element.22), calls=%async_computation.1 | async-start | bytes 2359296 | tf_op jit(solution)/shard_map/all_to_all | solution.py:42
  97.7 5.2 %collective-permute-start.11 = (bf16[432,128]{1,0:T(8,128)(2,1)S(1)}, bf16[432,128]{1,0:T(8,128)(2,1)S(1)}, u32[]{:S(2)}, u32[]{:S(2)}) collective-permute-start(bf16[432,128]{1,0:T(8,128)(2,1)S(1)} %get-tuple-element.24), channel_id=1, source_target_pairs={{0,1},{1,2},{2,3},{3,0},{4,5},{5,6},{6,7},{7,4},{8,9},{9,10},{10,1... | collective-permute-start | bytes 331784 | tf_op jit(solution)/shard_map/ppermute | solution.py:37
  98.0 7.2 %collective-permute-start.12 = (bf16[432,128]{1,0:T(8,128)(2,1)S(1)}, bf16[432,128]{1,0:T(8,128)(2,1)S(1)}, u32[]{:S(2)}, u32[]{:S(2)}) collective-permute-start(bf16[432,128]{1,0:T(8,128)(2,1)S(1)} %get-tuple-element.25), channel_id=1, source_target_pairs={{0,2},{1,3},{2,0},{3,1},{4,6},{5,7},{6,4},{7,5},{8,10},{9,11},{10,... | collective-permute-start | bytes 331784 | tf_op jit(solution)/shard_map/ppermute | solution.py:37
  101.8 3.6 %collective-permute-start.13 = (bf16[432,128]{1,0:T(8,128)(2,1)S(1)}, bf16[432,128]{1,0:T(8,128)(2,1)S(1)}, u32[]{:S(2)}, u32[]{:S(2)}) collective-permute-start(bf16[432,128]{1,0:T(8,128)(2,1)S(1)} %get-tuple-element.26), channel_id=1, source_target_pairs={{0,3},{1,0},{2,1},{3,2},{4,7},{5,4},{6,5},{7,6},{8,11},{9,8},{10,9... | collective-permute-start | bytes 331784 | tf_op jit(solution)/shard_map/ppermute | solution.py:37
  105.5 5.5 %collective-permute-start.16 = (bf16[208,128]{1,0:T(8,128)(2,1)S(1)}, bf16[208,128]{1,0:T(8,128)(2,1)S(1)}, u32[]{:S(2)}, u32[]{:S(2)}) collective-permute-start(bf16[208,128]{1,0:T(8,128)(2,1)S(1)} %shard_map.131.a_ref), channel_id=1, source_target_pairs={{0,3},{1,0},{2,1},{3,2},{4,7},{5,4},{6,5},{7,6},{8,11},{9,8},{10,9... | collective-permute-start | bytes 159752 | tf_op jit(solution)/shard_map/ppermute | solution.py:37
  107.2 5.4 %collective-permute-start.15 = (bf16[208,128]{1,0:T(8,128)(2,1)S(1)}, bf16[208,128]{1,0:T(8,128)(2,1)S(1)}, u32[]{:S(2)}, u32[]{:S(2)}) collective-permute-start(bf16[208,128]{1,0:T(8,128)(2,1)S(1)} %shard_map.131.a_ref), channel_id=1, source_target_pairs={{0,2},{1,3},{2,0},{3,1},{4,6},{5,7},{6,4},{7,5},{8,10},{9,11},{10,... | collective-permute-start | bytes 159752 | tf_op jit(solution)/shard_map/ppermute | solution.py:37
  107.2 6.2 %collective-permute-start.14 = (bf16[208,128]{1,0:T(8,128)(2,1)S(1)}, bf16[208,128]{1,0:T(8,128)(2,1)S(1)}, u32[]{:S(2)}, u32[]{:S(2)}) collective-permute-start(bf16[208,128]{1,0:T(8,128)(2,1)S(1)} %shard_map.131.a_ref), channel_id=1, source_target_pairs={{0,1},{1,2},{2,3},{3,0},{4,5},{5,6},{6,7},{7,4},{8,9},{9,10},{10,1... | collective-permute-start | bytes 159752 | tf_op jit(solution)/shard_map/ppermute | solution.py:37
  116.3 25.1 %all-to-all-start.2 = ((bf16[32,128,128]{2,1,0:T(8,128)(2,1)}), bf16[32,128,128]{2,1,0:T(8,128)(2,1)S(1)}, u32[]{:S(2)}, u32[]{:S(2)}) async-start(bf16[32,128,128]{2,1,0:T(8,128)(2,1)} %shard_map.132), calls=%async_computation.2 | async-start | bytes 2097152 | tf_op jit(solution)/shard_map/all_to_all | solution.py:42
  141.7 12.2 %collective-permute-start.17 = (bf16[64,128]{1,0:T(8,128)(2,1)S(1)}, bf16[64,128]{1,0:T(8,128)(2,1)S(1)}, u32[]{:S(2)}, u32[]{:S(2)}) collective-permute-start(bf16[64,128]{1,0:T(8,128)(2,1)S(1)} %get-tuple-element.33), channel_id=1, source_target_pairs={{0,4},{4,0},{8,12},{12,8},{16,20},{20,16},{24,28},{28,24},{32,36},... | collective-permute-start | bytes 49160 | tf_op jit(solution)/shard_map/ppermute | solution.py:33

commit v4 on v3

--- a/solution.py
+++ b/solution.py
@@ -136,6 +136,11 @@
         out_specs=[VMEM] * (QUARTERS - 1),
         scratch_shapes=[pltpu.SemaphoreType.DMA((QUARTERS - 1,))],
     )(place, in_hbm(weights))
+
+
+def repeat_kernel(value_ref, out_ref):
+    for p in range(PLANE):
+        out_ref[p] = value_ref[...]
 
 
 def in_hbm(value):
@@ -241,11 +246,17 @@
     for step, ref in enumerate((a_ref, b_ref, c_ref, d_ref)):
         start = pl.multiple_of(places_ref[step] * ref.shape[0], 16)
         hidden[pl.ds(start, ref.shape[0]), :] = ref[...]
-    values = hidden[...].astype(F32).T.astype(BF16)
+    units = own_ref.shape[0]
+    values = [
+        hidden[side * units : (side + 1) * units, :].astype(F32).T.astype(BF16)
+        for side in range(CORES)
+    ]
     for p in range(0, PLANE, 2):
         columns = slice(p * PAIR, (p + 2) * PAIR)
-        rows = jnp.concatenate([own_ref[:, columns], other_ref[:, columns]], 0)
-        part = jnp.dot(values, rows, preferred_element_type=F32).astype(BF16)
+        part = sum(
+            jnp.dot(value, ref[:, columns], preferred_element_type=F32)
+            for value, ref in zip(values, (own_ref, other_ref))
+        ).astype(BF16)
         out_ref[p] = part[:, :PAIR]
         out_ref[p + 1] = part[:, PAIR:]
 
@@ -295,7 +306,10 @@
     gain = pair_order(gain, received[:, half:], core)
 
     attended = attend(query, key_cache, value_cache, key_new, value_new, lengths)
-    gathered = plane_exchange(jnp.broadcast_to(attended[None], (PLANE,) + attended.shape))
+    (attended,) = kernel_call(
+        repeat_kernel, [pltpu.VMEM((PLANE,) + attended.shape, BF16)], scalars=0, inputs=1
+    )(attended)
+    gathered = plane_exchange(attended)
     rows = gathered.reshape(half, width)
 
     other_out = to_core(own_out)
@@ -318,7 +332,7 @@
         hsum_kernel,
         [
             jax.ShapeDtypeStruct((PAIR, HALF), F32),
-            jax.ShapeDtypeStruct((PLANE, PAIR + TAIL, HALF), BF16),
+            pltpu.VMEM((PLANE, PAIR + TAIL, HALF), BF16),
         ],
         scalars=0,
         inputs=6,
@@ -361,7 +375,7 @@
     places = ((source // 2) ^ core) * 2 + source % 2
     (branch,) = kernel_call(
         contract_kernel,
-        [jax.ShapeDtypeStruct((PLANE, HALF, PAIR), BF16)],
+        [pltpu.VMEM((PLANE, HALF, PAIR), BF16)],
         scratch=[pltpu.VMEM((4 * units, HALF), BF16)],
         inputs=6,
     )(places, *[held(w) for w in loaded(down_weight, down_other)], *chunks)

time: 155 us -> 155 us (level)
    pallas_call x2 -> x3, Pallas kernels: 3.96 us -> 5.04 us  [the longest x1 2.87 us: per_device(): kernel_call(contract_kernel, [pltpu.VMEM((PLANE, HALF, PAIR), BF16)], scr...]
  transfers between devices with their start and end apart: 21 -> 21, of which waited for: 14 -> 14; matrix products, arithmetic and copies ran while one was open for 8% -> 7% of each run, Pallas kernels for 7% -> 8%
where the time goes in v4:
time: 155 us; the launch traced here: 154 us
  waiting for transfers between devices  71.5 us (46%)
  starting transfers between devices  55 us (35%)
  Pallas kernels  16 us (10%)
  matrix products  6.23 us (4%)
  other arithmetic  3.44 us (2%)
  local copies, waits for them, and re-layouts  1.65 us (1%)
    all_to_all x3, waiting for transfers between devices, plane_exchange(): lax.all_to_all(blocks, 'gx', 0, 0, axis_index_groups=groups, tiled=True)  49.9 us
    all_to_all x3, starting transfers between devices, plane_exchange(): lax.all_to_all(blocks, 'gx', 0, 0, axis_index_groups=groups, tiled=True)  27.2 us
    ppermute x12, waiting for transfers between devices, along_gy(): lax.ppermute(value, 'gy', [(i, (i + step) % QUARTERS) for i in range(QUAR...  18.2 us
    ppermute x6, starting transfers between devices, to_core(): return lax.ppermute(value, 'gx', [(g, g ^ 1) for g in range(PLANE * CORES)])  14 us
    ppermute x12, starting transfers between devices, along_gy(): lax.ppermute(value, 'gy', [(i, (i + step) % QUARTERS) for i in range(QUAR...  13.9 us
    pallas_call x1, Pallas kernels, per_device(): kernel_call(expand_kernel, [message] * QUARTERS, scratch=[pltpu.VMEM((wid...  6.4 us
    dot_general x2, matrix products, project(): lax.dot_general(weights, rows, (((1,), (1,)), ((), ())), preferred_elemen...  4.58 us
    ppermute x6, waiting for transfers between devices, to_core(): return lax.ppermute(value, 'gx', [(g, g ^ 1) for g in range(PLANE * CORES)])  3.36 us
  transfers between devices with their start and end apart: 21, of which 14 were waited for; matrix products, arithmetic and copies ran while one was open for 7% of the time, Pallas kernels for 8%

profile of v4, /device:TPU:1, one launch (start us, length us, event | category | flops | bytes accessed | tf_op | source)
XLA Modules:
  0.0 154.3 jit_solution(14329917440014691341)
XLA Ops:
  0.0 1.5 shard_map.127
  1.5 2.1 %collective-permute-start = (bf16[64,4096]{1,0:T(8,128)(2,1)S(1)}, bf16[64,4096]{1,0:T(8,128)(2,1)}, u32[]{:S(2)}, u32[]{:S(2)}) collective-permute-start(bf16[64,4096]{1,0:T(8,128)(2,1)S(1)} %get-tuple-element.16), channel_id=1, source_target_pairs={{0,1},{1,2},{2,3},{3,0},{4,5},{5,6},{6,7},{7,4},{8,9},{9,10},{10,1... | collective-permute-start | bytes 1572872 | tf_op jit(solution)/shard_map/ppermute | solution.py:37
  3.6 2.5 %collective-permute-start.1 = (bf16[64,4096]{1,0:T(8,128)(2,1)S(1)}, bf16[64,4096]{1,0:T(8,128)(2,1)}, u32[]{:S(2)}, u32[]{:S(2)}) collective-permute-start(bf16[64,4096]{1,0:T(8,128)(2,1)S(1)} %get-tuple-element.17), channel_id=1, source_target_pairs={{0,2},{1,3},{2,0},{3,1},{4,6},{5,7},{6,4},{7,5},{8,10},{9,11},{10,... | collective-permute-start | bytes 1572872 | tf_op jit(solution)/shard_map/ppermute | solution.py:37
  6.1 1.2 collective-permute-start.2
  7.4 0.1 fusion.22
  7.5 0.3 fusion.21
  7.9 0.2 fusion.4
  8.1 0.2 fusion.2
  8.4 1.1 shard_map.128
  9.4 11.2 %all-to-all-start = ((bf16[32,4,4096]{2,1,0:T(4,128)(2,1)}), bf16[32,4,4096]{2,1,0:T(4,128)(2,1)S(1)}, u32[]{:S(2)}, u32[]{:S(2)}) async-start(bf16[32,4,4096]{2,1,0:T(4,128)(2,1)} %shard_map.128), calls=%async_computation | async-start | bytes 2097152 | tf_op jit(solution)/shard_map/all_to_all | solution.py:42
  20.6 1.1 dynamic-slice_bitcast_fusion
  21.8 7.0 %collective-permute-done.1 = bf16[64,4096]{1,0:T(8,128)(2,1)} collective-permute-done((bf16[64,4096]{1,0:T(8,128)(2,1)S(1)}, bf16[64,4096]{1,0:T(8,128)(2,1)}, u32[]{:S(2)}, u32[]{:S(2)}) %collective-permute-start.1) | collective-permute-done | bytes 524320 | tf_op jit(solution)/shard_map/ppermute | solution.py:37
  28.8 2.9 %pad_maximum_fusion = bf16[256,4096]{1,0:T(8,128)(2,1)} fusion(bf16[64,4096]{1,0:T(8,128)(2,1)} %collective-permute-done.2, bf16[64,4096]{1,0:T(8,128)(2,1)} %collective-permute-done.1, bf16[64,4096]{1,0:T(8,128)(2,1)} %collective-permute-done, bf16[64,4096]{1,0:T(8,128)(2,1)S(1)} %dynamic-slice_bitcast_fusion), kind=kLoop, calls=%fused_computation | loop fusion | flops 8388608 | bytes 4194304 | tf_op jit(solution)/shard_map/concatenate | solution.py:295
  31.7 1.5 %collective-permute-start.3 = (bf16[256,4096]{1,0:T(8,128)(2,1)}, bf16[256,4096]{1,0:T(8,128)(2,1)}, u32[]{:S(2)}, u32[]{:S(2)}) collective-permute-start(bf16[256,4096]{1,0:T(8,128)(2,1)} %pad_maximum_fusion), channel_id=1, source_target_pairs={{0,4},{4,0},{8,12},{12,8},{16,20},{20,16},{24,28},{28,24},{32,36},... | collective-permute-start | bytes 6291464 | tf_op jit(solution)/shard_map/ppermute | solution.py:33
  33.2 0.1 convolution_convert_fusion
  33.6 0.5 collective-permute-start.9
  34.2 0.4 collective-permute-start.8
  34.6 2.5 %collective-permute-done.7 = bf16[64,256]{1,0:T(8,128)(2,1)S(1)} collective-permute-done((bf16[64,256]{1,0:T(8,128)(2,1)S(1)}, bf16[64,256]{1,0:T(8,128)(2,1)S(1)}, u32[]{:S(2)}, u32[]{:S(2)}) %collective-permute-start.7) | collective-permute-done | bytes 32800 | tf_op jit(solution)/shard_map/ppermute | solution.py:33
  37.1 8.0 %all-to-all-done = bf16[32,4,4096]{2,1,0:T(4,128)(2,1)S(1)} async-done(((bf16[32,4,4096]{2,1,0:T(4,128)(2,1)}), bf16[32,4,4096]{2,1,0:T(4,128)(2,1)S(1)}, u32[]{:S(2)}, u32[]{:S(2)}) %all-to-all-start) | async-done | bytes 1048608 | tf_op jit(solution)/shard_map/all_to_all | solution.py:42
  45.1 0.3 reshape.66
  45.4 2.3 %fusion.23 = f32[4,64,128]{2,1,0:T(8,128)S(1)} fusion(bf16[4,64,4096]{2,1,0:T(8,128)(2,1)} %bitcast.3, bf16[128,4096,1]{1,0,2:T(8,128)(2,1)S(1)} %reshape.66), kind=kOutput, calls=%fused_computation.57 | convolution fusion | flops 268435456 | bytes 3276800 | tf_op jit(solution)/shard_map/dot_general | solution.py:318
  47.7 2.3 %fusion.24 = f32[4,64,128]{2,1,0:T(8,128)S(1)} fusion(bf16[4,64,4096]{2,1,0:T(8,128)(2,1)} %bitcast.6, bf16[128,4096,1]{1,0,2:T(8,128)(2,1)S(1)} %reshape.66), kind=kOutput, calls=%fused_computation.58 | convolution fusion | flops 268435456 | bytes 3276800 | tf_op jit(solution)/shard_map/dot_general | solution.py:318
  50.1 0.4 collective-permute-start.6
  50.5 1.1 collective-permute-start.5
  51.6 2.5 %collective-permute-done.6.c_ref = bf16[128,128]{1,0:T(8,128)(2,1)S(1)} collective-permute-done((bf16[128,128]{1,0:T(8,128)(2,1)S(1)}, bf16[128,128]{1,0:T(8,128)(2,1)S(1)}, u32[]{:S(2)}, u32[]{:S(2)}) %collective-permute-start.6) | collective-permute-done | bytes 32800 | tf_op jit(solution)/shard_map/ppermute | solution.py:37
  54.1 0.7 collective-permute-done.5.b_ref
  54.8 2.0 %collective-permute-done.4.a_ref = bf16[128,128]{1,0:T(8,128)(2,1)S(1)} collective-permute-done((bf16[128,128]{1,0:T(8,128)(2,1)S(1)}, bf16[128,128]{1,0:T(8,128)(2,1)S(1)}, u32[]{:S(2)}, u32[]{:S(2)}) %collective-permute-start.4) | collective-permute-done | bytes 32800 | tf_op jit(solution)/shard_map/ppermute | solution.py:37
  56.9 1.1 shard_map.129
  58.0 8.9 %all-to-all-start.1 = ((bf16[32,144,128]{2,1,0:T(8,128)(2,1)}), bf16[32,144,128]{2,1,0:T(8,128)(2,1)S(1)}, u32[]{:S(2)}, u32[]{:S(2)}) async-start(bf16[32,144,128]{2,1,0:T(8,128)(2,1)} %get-tuple-element.22), calls=%async_computation.1 | async-start | bytes 2359296 | tf_op jit(solution)/shard_map/all_to_all | solution.py:42
  66.9 23.9 %all-to-all-done.1.refs_4_ = bf16[32,144,128]{2,1,0:T(8,128)(2,1)S(1)} async-done(((bf16[32,144,128]{2,1,0:T(8,128)(2,1)}), bf16[32,144,128]{2,1,0:T(8,128)(2,1)S(1)}, u32[]{:S(2)}, u32[]{:S(2)}) %all-to-all-start.1) | async-done | bytes 1179680 | tf_op jit(solution)/shard_map/all_to_all | solution.py:42
  90.8 6.4 %shard_map.131 = (bf16[432,128]{1,0:T(8,128)(2,1)S(1)}, bf16[432,128]{1,0:T(8,128)(2,1)S(1)}, bf16[432,128]{1,0:T(8,128)(2,1)S(1)}, bf16[432,128]{1,0:T(8,128)(2,1)S(1)}) custom-call(s32[1]{0:T(128)} %bitcast.13.a_step, s32[1]{0:T(128)} %bitcast.14.b_step, s32[1]{0:T(128)} %bitcast.15.c_step, s32[1]{0:T(128)} %bitcast.16.d_step, bf16[416,4096]{1,0:T(8,128)(2,1)} %bitcast.54, ...), custom_call_target="tpu_custom_call" | custom-call | tf_op jit(solution)/shard_map/pallas_call | solution.py:348
  97.2 0.3 collective-permute-start.11
  97.6 3.9 %collective-permute-start.12 = (bf16[432,128]{1,0:T(8,128)(2,1)S(1)}, bf16[432,128]{1,0:T(8,128)(2,1)S(1)}, u32[]{:S(2)}, u32[]{:S(2)}) collective-permute-start(bf16[432,128]{1,0:T(8,128)(2,1)S(1)} %get-tuple-element.25), channel_id=1, source_target_pairs={{0,2},{1,3},{2,0},{3,1},{4,6},{5,7},{6,4},{7,5},{8,10},{9,11},{10,... | collective-permute-start | bytes 331784 | tf_op jit(solution)/shard_map/ppermute | solution.py:37
  101.5 1.0 collective-permute-done.11.b_ref
  102.4 2.4 %collective-permute-done.12.c_ref = bf16[432,128]{1,0:T(8,128)(2,1)S(1)} collective-permute-done((bf16[432,128]{1,0:T(8,128)(2,1)S(1)}, bf16[432,128]{1,0:T(8,128)(2,1)S(1)}, u32[]{:S(2)}, u32[]{:S(2)}) %collective-permute-start.12) | collective-permute-done | bytes 110624 | tf_op jit(solution)/shard_map/ppermute | solution.py:37
  104.8 0.3 collective-permute-done.13.d_ref
  105.2 1.7 %collective-permute-start.16 = (bf16[208,128]{1,0:T(8,128)(2,1)S(1)}, bf16[208,128]{1,0:T(8,128)(2,1)S(1)}, u32[]{:S(2)}, u32[]{:S(2)}) collective-permute-start(bf16[208,128]{1,0:T(8,128)(2,1)S(1)} %shard_map.132.a_ref), channel_id=1, source_target_pairs={{0,3},{1,0},{2,1},{3,2},{4,7},{5,4},{6,5},{7,6},{8,11},{9,8},{10,9... | collective-permute-start | bytes 159752 | tf_op jit(solution)/shard_map/ppermute | solution.py:37
  106.8 0.8 collective-permute-start.14
  107.6 3.0 %shard_map.130 = (bf16[416,4096]{1,0:T(8,128)(2,1)S(1)}, bf16[416,4096]{1,0:T(8,128)(2,1)S(1)}) custom-call(bf16[416,4096]{1,0:T(8,128)(2,1)} %refs_0_.1, bf16[416,4096]{1,0:T(8,128)(2,1)} %collective-permute-done.8.refs_1_), custom_call_target="tpu_custom_call" | custom-call | tf_op jit(solution)/shard_map/pallas_call | solution.py:162
  110.7 1.6 %collective-permute-done.15.c_ref = bf16[208,128]{1,0:T(8,128)(2,1)S(1)} collective-permute-done((bf16[208,128]{1,0:T(8,128)(2,1)S(1)}, bf16[208,128]{1,0:T(8,128)(2,1)S(1)}, u32[]{:S(2)}, u32[]{:S(2)}) %collective-permute-start.15) | collective-permute-done | bytes 53280 | tf_op jit(solution)/shard_map/ppermute | solution.py:37
  112.3 0.8 collective-permute-done.14.b_ref
  113.1 2.9 %shard_map.133 = bf16[32,128,128]{2,1,0:T(8,128)(2,1)} custom-call(s32[4]{0:T(128)S(1)} %fusion.15.places_ref, bf16[416,4096]{1,0:T(8,128)(2,1)S(1)} %get-tuple-element.20.own_ref, bf16[416,4096]{1,0:T(8,128)(2,1)S(1)} %get-tuple-element.21.other_ref, bf16[208,128]{1,0:T(8,128)(2,1)S(1)} %shard_map.132.a_ref, ...), custom_call_target="tpu_custom_call" | custom-call | tf_op jit(solution)/shard_map/pallas_call | solution.py:376
  115.9 7.1 %all-to-all-start.2 = ((bf16[32,128,128]{2,1,0:T(8,128)(2,1)}), bf16[32,128,128]{2,1,0:T(8,128)(2,1)S(1)}, u32[]{:S(2)}, u32[]{:S(2)}) async-start(bf16[32,128,128]{2,1,0:T(8,128)(2,1)} %shard_map.133), calls=%async_computation.2 | async-start | bytes 2097152 | tf_op jit(solution)/shard_map/all_to_all | solution.py:42
  123.0 18.0 %all-to-all-done.2 = bf16[32,128,128]{2,1,0:T(8,128)(2,1)S(1)} async-done(((bf16[32,128,128]{2,1,0:T(8,128)(2,1)}), bf16[32,128,128]{2,1,0:T(8,128)(2,1)S(1)}, u32[]{:S(2)}, u32[]{:S(2)}) %all-to-all-start.2) | async-done | bytes 1048608 | tf_op jit(solution)/shard_map/all_to_all | solution.py:42
  141.0 0.2 convert_reduce_fusion
  141.3 11.3 %collective-permute-start.17 = (bf16[64,128]{1,0:T(8,128)(2,1)S(1)}, bf16[64,128]{1,0:T(8,128)(2,1)S(1)}, u32[]{:S(2)}, u32[]{:S(2)}) collective-permute-start(bf16[64,128]{1,0:T(8,128)(2,1)S(1)} %get-tuple-element.33), channel_id=1, source_target_pairs={{0,4},{4,0},{8,12},{12,8},{16,20},{20,16},{24,28},{28,24},{32,36},... | collective-permute-start | bytes 49160 | tf_op jit(solution)/shard_map/ppermute | solution.py:33
  152.7 0.8 collective-permute-done.17
  153.5 0.8 fusion.3
  (50 shorter events, 0.8 us)
Async XLA Ops:
  0.0 7.5 %copy-start = (bf16[4,2,256,128]{3,2,1,0:T(8,128)(2,1)S(1)}, bf16[4,2,256,128]{3,2,1,0:T(8,128)(2,1)}, u32[]{:S(2)}) copy-start(bf16[4,2,256,128]{3,2,1,0:T(8,128)(2,1)} %param.14) | copy-start | bytes 1572868
  0.0 7.2 %copy-start.8 = (s32[4]{0:T(128)S(1)}, s32[4]{0:T(128)}, u32[]{:S(2)}) copy-start(s32[4]{0:T(128)} %param.18) | copy-start | bytes 52
  0.0 7.3 %copy-start.4 = (bf16[4,256]{1,0:T(4,128)(2,1)S(1)}, bf16[4,256]{1,0:T(4,128)(2,1)}, u32[]{:S(2)}) copy-start(bf16[4,256]{1,0:T(4,128)(2,1)} %param.16) | copy-start | bytes 6148
  0.0 7.3 %copy-start.5 = (bf16[4,256]{1,0:T(4,128)(2,1)S(1)}, bf16[4,256]{1,0:T(4,128)(2,1)}, u32[]{:S(2)}) copy-start(bf16[4,256]{1,0:T(4,128)(2,1)} %param.17) | copy-start | bytes 6148
  0.0 7.3 %copy-start.2 = (bf16[4,4096]{1,0:T(4,128)(2,1)S(1)}, bf16[4,4096]{1,0:T(4,128)(2,1)}, u32[]{:S(2)}) copy-start(bf16[4,4096]{1,0:T(4,128)(2,1)} %param.13) | copy-start | bytes 98308
  0.0 8.0 %copy-start.7 = (bf16[4,2,256,128]{3,2,1,0:T(8,128)(2,1)S(1)}, bf16[4,2,256,128]{3,2,1,0:T(8,128)(2,1)}, u32[]{:S(2)}) copy-start(bf16[4,2,256,128]{3,2,1,0:T(8,128)(2,1)} %param.15) | copy-start | bytes 1572868
  1.5 20.3 %collective-permute-start = (bf16[64,4096]{1,0:T(8,128)(2,1)S(1)}, bf16[64,4096]{1,0:T(8,128)(2,1)}, u32[]{:S(2)}, u32[]{:S(2)}) collective-permute-start(bf16[64,4096]{1,0:T(8,128)(2,1)S(1)} %get-tuple-element.16), channel_id=1, source_target_pairs={{0,1},{1,2},{2,3},{3,0},{4,5},{5,6},{6,7},{7,4},{8,9},{9,10},{10,1... | collective-permute-start | bytes 1572872 | tf_op jit(solution)/shard_map/ppermute | solution.py:37
  3.6 25.1 %collective-permute-start.1 = (bf16[64,4096]{1,0:T(8,128)(2,1)S(1)}, bf16[64,4096]{1,0:T(8,128)(2,1)}, u32[]{:S(2)}, u32[]{:S(2)}) collective-permute-start(bf16[64,4096]{1,0:T(8,128)(2,1)S(1)} %get-tuple-element.17), channel_id=1, source_target_pairs={{0,2},{1,3},{2,0},{3,1},{4,6},{5,7},{6,4},{7,5},{8,10},{9,11},{10,... | collective-permute-start | bytes 1572872 | tf_op jit(solution)/shard_map/ppermute | solution.py:37
  6.1 22.7 %collective-permute-start.2 = (bf16[64,4096]{1,0:T(8,128)(2,1)S(1)}, bf16[64,4096]{1,0:T(8,128)(2,1)}, u32[]{:S(2)}, u32[]{:S(2)}) collective-permute-start(bf16[64,4096]{1,0:T(8,128)(2,1)S(1)} %get-tuple-element.18), channel_id=1, source_target_pairs={{0,3},{1,0},{2,1},{3,2},{4,7},{5,4},{6,5},{7,6},{8,11},{9,8},{10,9... | collective-permute-start | bytes 1572872 | tf_op jit(solution)/shard_map/ppermute | solution.py:37
  9.4 35.7 %all-to-all-start = ((bf16[32,4,4096]{2,1,0:T(4,128)(2,1)}), bf16[32,4,4096]{2,1,0:T(4,128)(2,1)S(1)}, u32[]{:S(2)}, u32[]{:S(2)}) async-start(bf16[32,4,4096]{2,1,0:T(4,128)(2,1)} %shard_map.128), calls=%async_computation | async-start | bytes 2097152 | tf_op jit(solution)/shard_map/all_to_all | solution.py:42
  21.7 11.5 %copy-start.1 = (bf16[256,256]{1,0:T(8,128)(2,1)S(1)}, bf16[256,256]{1,0:T(8,128)(2,1)}, u32[]{:S(2)}) copy-start(bf16[256,256]{1,0:T(8,128)(2,1)} %constant.92.clone) | copy-start | bytes 393220
  21.7 11.5 %copy-start.3 = (bf16[256,64]{0,1:T(8,128)(2,1)S(1)}, bf16[256,64]{0,1:T(8,128)(2,1)}, u32[]{:S(2)}) copy-start(bf16[256,64]{0,1:T(8,128)(2,1)} %param.19) | copy-start | bytes 98308
  21.8 11.6 %copy-start.6 = (bf16[64]{0:T(256)(128)(2,1)S(1)}, bf16[64]{0:T(256)(128)(2,1)}, u32[]{:S(2)}) copy-start(bf16[64]{0:T(256)(128)(2,1)} %param.21) | copy-start | bytes 388
  31.7 16.0 %collective-permute-start.3 = (bf16[256,4096]{1,0:T(8,128)(2,1)}, bf16[256,4096]{1,0:T(8,128)(2,1)}, u32[]{:S(2)}, u32[]{:S(2)}) collective-permute-start(bf16[256,4096]{1,0:T(8,128)(2,1)} %pad_maximum_fusion), channel_id=1, source_target_pairs={{0,4},{4,0},{8,12},{12,8},{16,20},{20,16},{24,28},{28,24},{32,36},... | collective-permute-start | bytes 6291464 | tf_op jit(solution)/shard_map/ppermute | solution.py:33
  33.5 3.6 %collective-permute-start.7 = (bf16[64,256]{1,0:T(8,128)(2,1)S(1)}, bf16[64,256]{1,0:T(8,128)(2,1)S(1)}, u32[]{:S(2)}, u32[]{:S(2)}) collective-permute-start(bf16[64,256]{1,0:T(8,128)(2,1)S(1)} %pad_maximum_fusion.1), channel_id=1, source_target_pairs={{0,4},{4,0},{8,12},{12,8},{16,20},{20,16},{24,28},{28,24},{32,36},... | collective-permute-start | bytes 98312 | tf_op jit(solution)/shard_map/ppermute | solution.py:33
  33.6 33.3 %collective-permute-start.9 = (bf16[416,4096]{1,0:T(8,128)(2,1)}, bf16[416,4096]{1,0:T(8,128)(2,1)}, u32[]{:S(2)}, u32[]{:S(2)}) collective-permute-start(bf16[416,4096]{1,0:T(8,128)(2,1)} %bitcast.53), channel_id=1, source_target_pairs={{0,4},{4,0},{8,12},{12,8},{16,20},{20,16},{24,28},{28,24},{32,36},... | collective-permute-start | bytes 10223624 | tf_op jit(solution)/shard_map/ppermute | solution.py:33
  34.1 32.9 %collective-permute-start.10 = (bf16[416,4096]{1,0:T(8,128)(2,1)}, bf16[416,4096]{1,0:T(8,128)(2,1)}, u32[]{:S(2)}, u32[]{:S(2)}) collective-permute-start(bf16[416,4096]{1,0:T(8,128)(2,1)} %bitcast.55), channel_id=1, source_target_pairs={{0,4},{4,0},{8,12},{12,8},{16,20},{20,16},{24,28},{28,24},{32,36},... | collective-permute-start | bytes 10223624 | tf_op jit(solution)/shard_map/ppermute | solution.py:33
  34.2 73.4 %collective-permute-start.8 = (bf16[416,4096]{1,0:T(8,128)(2,1)}, bf16[416,4096]{1,0:T(8,128)(2,1)}, u32[]{:S(2)}, u32[]{:S(2)}) collective-permute-start(bf16[416,4096]{1,0:T(8,128)(2,1)} %refs_0_.1), channel_id=1, source_target_pairs={{0,4},{4,0},{8,12},{12,8},{16,20},{20,16},{24,28},{28,24},{32,36},... | collective-permute-start | bytes 10223624 | tf_op jit(solution)/shard_map/ppermute | solution.py:33
  50.1 4.1 %collective-permute-start.6 = (bf16[128,128]{1,0:T(8,128)(2,1)S(1)}, bf16[128,128]{1,0:T(8,128)(2,1)S(1)}, u32[]{:S(2)}, u32[]{:S(2)}) collective-permute-start(bf16[128,128]{1,0:T(8,128)(2,1)S(1)} %get-tuple-element.29), channel_id=1, source_target_pairs={{0,1},{1,2},{2,3},{3,0},{4,5},{5,6},{6,7},{7,4},{8,9},{9,10},{10,1... | collective-permute-start | bytes 98312 | tf_op jit(solution)/shard_map/ppermute | solution.py:37
  50.5 4.4 %collective-permute-start.5 = (bf16[128,128]{1,0:T(8,128)(2,1)S(1)}, bf16[128,128]{1,0:T(8,128)(2,1)S(1)}, u32[]{:S(2)}, u32[]{:S(2)}) collective-permute-start(bf16[128,128]{1,0:T(8,128)(2,1)S(1)} %get-tuple-element.30), channel_id=1, source_target_pairs={{0,2},{1,3},{2,0},{3,1},{4,6},{5,7},{6,4},{7,5},{8,10},{9,11},{10,... | collective-permute-start | bytes 98312 | tf_op jit(solution)/shard_map/ppermute | solution.py:37
  54.1 2.8 %collective-permute-start.4 = (bf16[128,128]{1,0:T(8,128)(2,1)S(1)}, bf16[128,128]{1,0:T(8,128)(2,1)S(1)}, u32[]{:S(2)}, u32[]{:S(2)}) collective-permute-start(bf16[128,128]{1,0:T(8,128)(2,1)S(1)} %get-tuple-element.31), channel_id=1, source_target_pairs={{0,3},{1,0},{2,1},{3,2},{4,7},{5,4},{6,5},{7,6},{8,11},{9,8},{10,9... | collective-permute-start | bytes 98312 | tf_op jit(solution)/shard_map/ppermute | solution.py:37
  58.0 32.8 %all-to-all-start.1 = ((bf16[32,144,128]{2,1,0:T(8,128)(2,1)}), bf16[32,144,128]{2,1,0:T(8,128)(2,1)S(1)}, u32[]{:S(2)}, u32[]{:S(2)}) async-start(bf16[32,144,128]{2,1,0:T(8,128)(2,1)} %get-tuple-element.22), calls=%async_computation.1 | async-start | bytes 2359296 | tf_op jit(solution)/shard_map/all_to_all | solution.py:42
  97.2 5.2 %collective-permute-start.11 = (bf16[432,128]{1,0:T(8,128)(2,1)S(1)}, bf16[432,128]{1,0:T(8,128)(2,1)S(1)}, u32[]{:S(2)}, u32[]{:S(2)}) collective-permute-start(bf16[432,128]{1,0:T(8,128)(2,1)S(1)} %get-tuple-element.24), channel_id=1, source_target_pairs={{0,1},{1,2},{2,3},{3,0},{4,5},{5,6},{6,7},{7,4},{8,9},{9,10},{10,1... | collective-permute-start | bytes 331784 | tf_op jit(solution)/shard_map/ppermute | solution.py:37
  97.6 7.2 %collective-permute-start.12 = (bf16[432,128]{1,0:T(8,128)(2,1)S(1)}, bf16[432,128]{1,0:T(8,128)(2,1)S(1)}, u32[]{:S(2)}, u32[]{:S(2)}) collective-permute-start(bf16[432,128]{1,0:T(8,128)(2,1)S(1)} %get-tuple-element.25), channel_id=1, source_target_pairs={{0,2},{1,3},{2,0},{3,1},{4,6},{5,7},{6,4},{7,5},{8,10},{9,11},{10,... | collective-permute-start | bytes 331784 | tf_op jit(solution)/shard_map/ppermute | solution.py:37
  101.5 3.6 %collective-permute-start.13 = (bf16[432,128]{1,0:T(8,128)(2,1)S(1)}, bf16[432,128]{1,0:T(8,128)(2,1)S(1)}, u32[]{:S(2)}, u32[]{:S(2)}) collective-permute-start(bf16[432,128]{1,0:T(8,128)(2,1)S(1)} %get-tuple-element.26), channel_id=1, source_target_pairs={{0,3},{1,0},{2,1},{3,2},{4,7},{5,4},{6,5},{7,6},{8,11},{9,8},{10,9... | collective-permute-start | bytes 331784 | tf_op jit(solution)/shard_map/ppermute | solution.py:37
  105.2 5.5 %collective-permute-start.16 = (bf16[208,128]{1,0:T(8,128)(2,1)S(1)}, bf16[208,128]{1,0:T(8,128)(2,1)S(1)}, u32[]{:S(2)}, u32[]{:S(2)}) collective-permute-start(bf16[208,128]{1,0:T(8,128)(2,1)S(1)} %shard_map.132.a_ref), channel_id=1, source_target_pairs={{0,3},{1,0},{2,1},{3,2},{4,7},{5,4},{6,5},{7,6},{8,11},{9,8},{10,9... | collective-permute-start | bytes 159752 | tf_op jit(solution)/shard_map/ppermute | solution.py:37
  106.8 5.4 %collective-permute-start.15 = (bf16[208,128]{1,0:T(8,128)(2,1)S(1)}, bf16[208,128]{1,0:T(8,128)(2,1)S(1)}, u32[]{:S(2)}, u32[]{:S(2)}) collective-permute-start(bf16[208,128]{1,0:T(8,128)(2,1)S(1)} %shard_map.132.a_ref), channel_id=1, source_target_pairs={{0,2},{1,3},{2,0},{3,1},{4,6},{5,7},{6,4},{7,5},{8,10},{9,11},{10,... | collective-permute-start | bytes 159752 | tf_op jit(solution)/shard_map/ppermute | solution.py:37
  106.8 6.2 %collective-permute-start.14 = (bf16[208,128]{1,0:T(8,128)(2,1)S(1)}, bf16[208,128]{1,0:T(8,128)(2,1)S(1)}, u32[]{:S(2)}, u32[]{:S(2)}) collective-permute-start(bf16[208,128]{1,0:T(8,128)(2,1)S(1)} %shard_map.132.a_ref), channel_id=1, source_target_pairs={{0,1},{1,2},{2,3},{3,0},{4,5},{5,6},{6,7},{7,4},{8,9},{9,10},{10,1... | collective-permute-start | bytes 159752 | tf_op jit(solution)/shard_map/ppermute | solution.py:37
  115.9 25.1 %all-to-all-start.2 = ((bf16[32,128,128]{2,1,0:T(8,128)(2,1)}), bf16[32,128,128]{2,1,0:T(8,128)(2,1)S(1)}, u32[]{:S(2)}, u32[]{:S(2)}) async-start(bf16[32,128,128]{2,1,0:T(8,128)(2,1)} %shard_map.133), calls=%async_computation.2 | async-start | bytes 2097152 | tf_op jit(solution)/shard_map/all_to_all | solution.py:42
  141.3 12.2 %collective-permute-start.17 = (bf16[64,128]{1,0:T(8,128)(2,1)S(1)}, bf16[64,128]{1,0:T(8,128)(2,1)S(1)}, u32[]{:S(2)}, u32[]{:S(2)}) collective-permute-start(bf16[64,128]{1,0:T(8,128)(2,1)S(1)} %get-tuple-element.33), channel_id=1, source_target_pairs={{0,4},{4,0},{8,12},{12,8},{16,20},{20,16},{24,28},{28,24},{32,36},... | collective-permute-start | bytes 49160 | tf_op jit(solution)/shard_map/ppermute | solution.py:33
